TPU v7x, 768 devices: a whole 4x8x12 slice. The times are simulated.
768 devices in a mesh: dom: 96 (over z, y), sub: 8 (over x, core).
Axes of the slice: x: 4, y: 8, z: 12, core: 2. Of those that a mesh axis runs over, the one named last changes fastest.
Arguments:
- feats: bfloat16 [768, 393216], P('sub', 'dom'), may hold values from -6 to 6
- weight: bfloat16 [768, 768], replicated, may hold values from -0.21875 to 0.21875
- edge_dst: int32 [96, 64], P('dom'), may hold values from 0 to 31
- edge_src: int32 [96, 64], P('dom'), may hold values from 0 to 47, as said below
- edge_mask: int32 [96, 64, 128, 128], P('dom'), may hold values from 0 to 1
- send_list: int32 [96, 4, 4], P('dom'), may hold values from 0 to 31
- send_count: int32 [96, 4], P('dom'), may hold values from 1 to 4, as said below
- cotangent: bfloat16 [768, 393216], P(None, ('dom', 'sub')), may hold values from -6 to 6
Outputs:
- hidden: bfloat16 [768, 393216], P(None, ('dom', 'sub'))
- d_feats: bfloat16 [768, 393216], P('sub', 'dom')
- d_weight: float32 [768, 768], replicated
Inputs may be any that keep to these rules, and one draw needn't show every extreme that they name: `edge_src`: A tile 32 + j * 4 + k of partition p is read only where k < send_count[(p - r_j) mod 96, j]. Slots from send_count on are padding.
All inputs are finite; a program needn't handle non-finite values.
Results may differ from a plain program's by a relative error of at most 0.0068.
Values may be sent and summed in bfloat16 or wider, within the bound.
A program may use at most 64 MiB of HBM per device.

v0:
```python
import jax
import jax.numpy as jnp
from jax import lax
from jax.sharding import PartitionSpec as P


def passed_along(array, axis, by):
    devices = lax.axis_size(axis)
    return lax.ppermute(array, axis, [(i, (i + by) % devices) for i in range(devices)])


def offset_of(position):
    return (position // 2 + 1) * (1 - 2 * (position % 2))


def cycle_move(grad_piece, distance):
    return passed_along(grad_piece, "dom", distance)


def shards(feats, weight, edge_dst, edge_src, edge_mask, send_list, send_count, cotangent):
    highest = lax.Precision.HIGHEST
    columns, label_span = feats.shape
    tile_len = edge_mask.shape[2]
    block_count = label_span // tile_len
    offset_count = send_list.shape[1]
    capacity = send_list.shape[2]
    table_len = block_count + offset_count * capacity
    own_tiles = feats.reshape(columns, block_count, tile_len)
    targets = edge_dst[0]
    sources = edge_src[0]
    tile_masks = edge_mask[0].astype(jnp.bfloat16)
    slot_live = jnp.arange(capacity)[None, :] < send_count[0][:, None]
    chosen = jnp.take(own_tiles, send_list[0], axis=1)
    chosen = jnp.where(slot_live[None, :, :, None], chosen, jnp.zeros_like(chosen))
    arrived = [
        cycle_move(chosen[:, position], offset_of(position)) for position in range(offset_count)
    ]
    target_hot = jax.nn.one_hot(targets, block_count, dtype=jnp.float32)
    row_counts = jnp.sum(edge_mask[0], axis=2).astype(jnp.float32)
    degree = jnp.einsum("ep,eb->bp", row_counts, target_hot, precision=highest)
    row_scale = lax.rsqrt(1.0 + degree)
    source_table = jnp.concatenate([own_tiles] + arrived, axis=1)
    gathered = jnp.take(source_table, sources, axis=1)
    products = jnp.einsum("ceq,epq->cep", gathered, tile_masks, preferred_element_type=jnp.float32)
    summed = jnp.einsum("cep,eb->cbp", products, target_hot, precision=highest)
    aggregated = (
        ((own_tiles.astype(jnp.float32) + summed) * row_scale[None])
        .astype(jnp.bfloat16)
        .reshape(columns, label_span)
    )
    full_rows = lax.all_to_all(aggregated, "sub", split_axis=1, concat_axis=0, tiled=True)
    pre_act = jnp.dot(weight, full_rows, preferred_element_type=jnp.float32)
    hidden = jax.nn.silu(pre_act).astype(jnp.bfloat16)
    sigmoid_pre = jax.nn.sigmoid(pre_act)
    d_pre = (
        cotangent.astype(jnp.float32) * sigmoid_pre * (1.0 + pre_act * (1.0 - sigmoid_pre))
    ).astype(jnp.bfloat16)
    d_full = jnp.einsum("ok,ol->kl", weight, d_pre, preferred_element_type=jnp.float32).astype(
        jnp.bfloat16
    )
    back_cols = lax.all_to_all(d_full, "sub", split_axis=0, concat_axis=1, tiled=True)
    local_term = jnp.einsum("ol,kl->ok", d_pre, full_rows, preferred_element_type=jnp.float32)
    d_weight = lax.psum(local_term, ("dom", "sub"))
    scaled = (
        back_cols.reshape(columns, block_count, tile_len).astype(jnp.float32) * row_scale[None]
    ).astype(jnp.bfloat16)
    by_edge = jnp.take(scaled, targets, axis=1)
    d_source = jnp.einsum("cep,epq->ceq", by_edge, tile_masks, preferred_element_type=jnp.float32)
    source_hot = jax.nn.one_hot(sources, table_len, dtype=jnp.float32)
    d_table = jnp.einsum("ceq,et->ctq", d_source, source_hot, precision=highest)
    returned = []
    for position in range(offset_count):
        offset_start = block_count + position * capacity
        grad_piece = d_table[:, offset_start : offset_start + capacity].astype(jnp.bfloat16)
        returned.append(cycle_move(grad_piece, -offset_of(position)))
    returned_all = jnp.stack(returned, axis=1)
    send_hot = jax.nn.one_hot(send_list[0], block_count, dtype=jnp.bfloat16) * slot_live[
        :, :, None
    ].astype(jnp.bfloat16)
    back_sum = jnp.einsum(
        "cjkq,jkb->cbq", returned_all, send_hot, preferred_element_type=jnp.float32
    )
    d_feats = (
        (scaled.astype(jnp.float32) + d_table[:, :block_count] + back_sum)
        .astype(jnp.bfloat16)
        .reshape(columns, label_span)
    )
    return (hidden, d_feats, d_weight)


def solution(mesh):
    return jax.shard_map(
        shards,
        mesh=mesh,
        in_specs=(
            P("sub", "dom"),
            P(),
            P("dom", None),
            P("dom", None),
            P("dom", None, None, None),
            P("dom", None, None),
            P("dom", None),
            P(None, ("dom", "sub")),
        ),
        out_specs=(P(None, ("dom", "sub")), P("sub", "dom"), P()),
        check_vma=False,
    )
```

profile of v0, /device:TPU:1, one launch (start us, length us, event | category | flops | bytes accessed | tf_op | source)
XLA Modules:
  0.0 573.6 jit_solution(6360025737015151211)
XLA Ops:
  10.4 4.0 collective-permute-start
  14.5 15.9 %collective-permute-start.1 = (bf16[96,4,128]{2,1,0:T(4,128)(2,1)S(1)}, bf16[96,4,128]{2,1,0:T(4,128)(2,1)S(1)}, u32[]{:S(2)}, u32[]{:S(2)}) collective-permute-start(bf16[96,4,128]{2,1,0:T(4,128)(2,1)S(1)} %get-tuple-element.17), channel_id=1, source_target_pairs={{0,760},{8,0},{16,8},{24,16},{32,24},{40,32},{48,40},{56,48},{64,5... | collective-permute-start | bytes 294920 | tf_op jit(solution)/shard_map/ppermute | solution.py:9
  30.4 1.9 collective-permute-start.2
  32.3 7.6 %collective-permute-start.3 = (bf16[96,4,128]{2,1,0:T(4,128)(2,1)S(1)}, bf16[96,4,128]{2,1,0:T(4,128)(2,1)S(1)}, u32[]{:S(2)}, u32[]{:S(2)}) collective-permute-start(bf16[96,4,128]{2,1,0:T(4,128)(2,1)S(1)} %get-tuple-element.15), channel_id=1, source_target_pairs={{0,752},{8,760},{16,0},{24,8},{32,16},{40,24},{48,32},{56,40},{64,... | collective-permute-start | bytes 294920 | tf_op jit(solution)/shard_map/ppermute | solution.py:9
  41.2 3.3 reduce_sum.9
  45.3 3.7 concatenate.3
  50.6 2.1 gather_fusion.1
  52.7 4.3 fusion.8
  57.0 3.3 fusion.24
  61.9 5.8 %all-to-all-start = ((bf16[96,8,512]{2,0,1:T(8,128)(2,1)}), bf16[96,8,512]{2,0,1:T(8,128)(2,1)S(1)}, u32[]{:S(2)}, u32[]{:S(2)}) async-start(bf16[96,8,512]{2,0,1:T(8,128)(2,1)} %copy.18), calls=%async_computation | async-start | bytes 1572864 | tf_op jit(solution)/shard_map/all_to_all | solution.py:51
  68.0 12.0 %all-to-all-done = bf16[96,8,512]{2,0,1:T(8,128)(2,1)S(1)} async-done(((bf16[96,8,512]{2,0,1:T(8,128)(2,1)}), bf16[96,8,512]{2,0,1:T(8,128)(2,1)S(1)}, u32[]{:S(2)}, u32[]{:S(2)}) %all-to-all-start) | async-done | bytes 786464 | tf_op jit(solution)/shard_map/all_to_all | solution.py:51
  80.0 2.1 fusion.22
  84.1 4.3 all-to-all-start.1
  90.9 2.3 fusion.70
  93.2 7.6 %all-to-all-done.1 = bf16[8,96,512]{2,1,0:T(8,128)(2,1)S(1)} async-done(((bf16[8,96,512]{2,1,0:T(8,128)(2,1)}), bf16[8,96,512]{2,1,0:T(8,128)(2,1)S(1)}, u32[]{:S(2)}, u32[]{:S(2)}) %all-to-all-start.1) | async-done | bytes 786464 | tf_op jit(solution)/shard_map/all_to_all | solution.py:61
  101.0 2.1 copy.21
  106.9 3.0 fusion.6
  109.9 4.8 fusion.69
  114.9 2.1 collective-permute-start.7
  117.0 7.6 %collective-permute-start.6 = (bf16[96,4,128]{2,1,0:T(4,128)(2,1)S(1)}, bf16[96,4,128]{2,1,0:T(4,128)(2,1)S(1)}, u32[]{:S(2)}, u32[]{:S(2)}) collective-permute-start(bf16[96,4,128]{2,1,0:T(4,128)(2,1)S(1)} %get-tuple-element.13), channel_id=1, source_target_pairs={{0,752},{8,760},{16,0},{24,8},{32,16},{40,24},{48,32},{56,40},{64,... | collective-permute-start | bytes 294920 | tf_op jit(solution)/shard_map/ppermute | solution.py:9
  126.5 6.7 %collective-permute-start.4 = (bf16[96,4,128]{2,1,0:T(4,128)(2,1)S(1)}, bf16[96,4,128]{2,1,0:T(4,128)(2,1)S(1)}, u32[]{:S(2)}, u32[]{:S(2)}) collective-permute-start(bf16[96,4,128]{2,1,0:T(4,128)(2,1)S(1)} %get-tuple-element.11), channel_id=1, source_target_pairs={{0,760},{8,0},{16,8},{24,16},{32,24},{40,32},{48,40},{56,48},{64,5... | collective-permute-start | bytes 294920 | tf_op jit(solution)/shard_map/ppermute | solution.py:9
  134.8 2.1 fusion.14
  138.1 425.4 %all-reduce.2.cloned.1.call-done = f32[768,768]{1,0:T(8,128)} async-done(((f32[768,768]{1,0:T(8,128)}), f32[768,768]{1,0:T(8,128)}) %all-reduce.2.cloned.1.call-update) | async-done | bytes 2359312 | tf_op jit(solution)/shard_map/psum | solution.py:63
  563.5 3.2 copy.54
  (75 shorter events, 21.9 us)
Async XLA Ops:
  7.2 72.9 %copy-start = (bf16[768,768]{1,0:T(8,128)(2,1)S(1)}, bf16[768,768]{1,0:T(8,128)(2,1)}, u32[]{:S(2)}) copy-start(bf16[768,768]{1,0:T(8,128)(2,1)} %param.9) | copy-start | bytes 3538948
  8.6 31.3 %copy-start.15 = (s32[1,64]{1,0:T(1,128)S(1)}, s32[1,64]{1,0:T(1,128)}, u32[]{:S(2)}) copy-start(s32[1,64]{1,0:T(1,128)} %param.11) | copy-start | bytes 772
  8.6 32.4 %copy-start.1 = (bf16[96,4096]{1,0:T(8,128)(2,1)S(1)}, bf16[96,4096]{1,0:T(8,128)(2,1)}, u32[]{:S(2)}) copy-start(bf16[96,4096]{1,0:T(8,128)(2,1)} %param.8) | copy-start | bytes 2359300
  10.4 34.9 %collective-permute-start = (bf16[96,4,128]{2,1,0:T(4,128)(2,1)S(1)}, bf16[96,4,128]{2,1,0:T(4,128)(2,1)S(1)}, u32[]{:S(2)}, u32[]{:S(2)}) collective-permute-start(bf16[96,4,128]{2,1,0:T(4,128)(2,1)S(1)} %get-tuple-element.18), channel_id=1, source_target_pairs={{0,8},{8,16},{16,24},{24,32},{32,40},{40,48},{48,56},{56,64},{64,7... | collective-permute-start | bytes 294920 | tf_op jit(solution)/shard_map/ppermute | solution.py:9
  14.5 30.8 %collective-permute-start.1 = (bf16[96,4,128]{2,1,0:T(4,128)(2,1)S(1)}, bf16[96,4,128]{2,1,0:T(4,128)(2,1)S(1)}, u32[]{:S(2)}, u32[]{:S(2)}) collective-permute-start(bf16[96,4,128]{2,1,0:T(4,128)(2,1)S(1)} %get-tuple-element.17), channel_id=1, source_target_pairs={{0,760},{8,0},{16,8},{24,16},{32,24},{40,32},{48,40},{56,48},{64,5... | collective-permute-start | bytes 294920 | tf_op jit(solution)/shard_map/ppermute | solution.py:9
  30.4 14.9 %collective-permute-start.2 = (bf16[96,4,128]{2,1,0:T(4,128)(2,1)S(1)}, bf16[96,4,128]{2,1,0:T(4,128)(2,1)S(1)}, u32[]{:S(2)}, u32[]{:S(2)}) collective-permute-start(bf16[96,4,128]{2,1,0:T(4,128)(2,1)S(1)} %get-tuple-element.16), channel_id=1, source_target_pairs={{0,16},{8,24},{16,32},{24,40},{32,48},{40,56},{48,64},{56,72},{64,... | collective-permute-start | bytes 294920 | tf_op jit(solution)/shard_map/ppermute | solution.py:9
  32.3 13.0 %collective-permute-start.3 = (bf16[96,4,128]{2,1,0:T(4,128)(2,1)S(1)}, bf16[96,4,128]{2,1,0:T(4,128)(2,1)S(1)}, u32[]{:S(2)}, u32[]{:S(2)}) collective-permute-start(bf16[96,4,128]{2,1,0:T(4,128)(2,1)S(1)} %get-tuple-element.15), channel_id=1, source_target_pairs={{0,752},{8,760},{16,0},{24,8},{32,16},{40,24},{48,32},{56,40},{64,... | collective-permute-start | bytes 294920 | tf_op jit(solution)/shard_map/ppermute | solution.py:9
  41.1 3.4 copy-start.8
  41.1 3.5 copy-start.14
  50.6 2.2 copy-start.11
  52.7 4.3 copy-start.9
  60.8 6.9 %copy-start.4 = (bf16[768,512]{1,0:T(8,128)(2,1)S(1)}, bf16[768,512]{1,0:T(8,128)(2,1)}, u32[]{:S(2)}) copy-start(bf16[768,512]{1,0:T(8,128)(2,1)} %param.15) | copy-start | bytes 2359300
  61.9 18.1 %all-to-all-start = ((bf16[96,8,512]{2,0,1:T(8,128)(2,1)}), bf16[96,8,512]{2,0,1:T(8,128)(2,1)S(1)}, u32[]{:S(2)}, u32[]{:S(2)}) async-start(bf16[96,8,512]{2,0,1:T(8,128)(2,1)} %copy.18), calls=%async_computation | async-start | bytes 1572864 | tf_op jit(solution)/shard_map/all_to_all | solution.py:51
  84.1 16.6 %all-to-all-start.1 = ((bf16[8,96,512]{2,1,0:T(8,128)(2,1)}), bf16[8,96,512]{2,1,0:T(8,128)(2,1)S(1)}, u32[]{:S(2)}, u32[]{:S(2)}) async-start(bf16[8,96,512]{2,1,0:T(8,128)(2,1)} %bitcast.22), calls=%async_computation.1 | async-start | bytes 1572864 | tf_op jit(solution)/shard_map/all_to_all | solution.py:61
  88.4 475.1 %all-reduce.2.cloned.1.call-start = ((), (), s32[]{:S(2)}) async-start(), calls=%async_computation.2 | async-start | bytes 4718592 | tf_op jit(solution)/shard_map/psum | solution.py:63
  106.9 3.0 copy-start.16
  109.9 23.3 %copy-start.5 = (bf16[768,512]{0,1:T(8,128)(2,1)S(1)}, bf16[768,512]{0,1:T(8,128)(2,1)}, u32[]{:S(2)}) copy-start(bf16[768,512]{0,1:T(8,128)(2,1)} %get-tuple-element.10) | copy-start | bytes 2359300
  114.8 20.1 %copy-start.3 = (bf16[96,32,128]{2,1,0:T(8,128)(2,1)S(1)}, bf16[96,32,128]{2,1,0:T(8,128)(2,1)}, u32[]{:S(2)}) copy-start(bf16[96,32,128]{2,1,0:T(8,128)(2,1)} %copy-done.2) | copy-start | bytes 2359300
  114.8 20.1 %copy-start.7 = (s32[1,4,4]{2,1,0:T(4,128)S(1)}, s32[1,4,4]{2,1,0:T(4,128)}, u32[]{:S(2)}) copy-start(s32[1,4,4]{2,1,0:T(4,128)} %param.13) | copy-start | bytes 196
  114.8 20.1 %copy-start.10 = (bf16[4,4]{1,0:T(4,128)(2,1)S(1)}, bf16[4,4]{1,0:T(4,128)(2,1)}, u32[]{:S(2)}) copy-start(bf16[4,4]{1,0:T(4,128)(2,1)} %get-tuple-element.19) | copy-start | bytes 100
  114.9 19.4 %collective-permute-start.7 = (bf16[96,4,128]{2,1,0:T(4,128)(2,1)S(1)}, bf16[96,4,128]{2,1,0:T(4,128)(2,1)S(1)}, u32[]{:S(2)}, u32[]{:S(2)}) collective-permute-start(bf16[96,4,128]{2,1,0:T(4,128)(2,1)S(1)} %get-tuple-element.12), channel_id=1, source_target_pairs={{0,16},{8,24},{16,32},{24,40},{32,48},{40,56},{48,64},{56,72},{64,... | collective-permute-start | bytes 294920 | tf_op jit(solution)/shard_map/ppermute | solution.py:9
  117.0 17.4 %collective-permute-start.6 = (bf16[96,4,128]{2,1,0:T(4,128)(2,1)S(1)}, bf16[96,4,128]{2,1,0:T(4,128)(2,1)S(1)}, u32[]{:S(2)}, u32[]{:S(2)}) collective-permute-start(bf16[96,4,128]{2,1,0:T(4,128)(2,1)S(1)} %get-tuple-element.13), channel_id=1, source_target_pairs={{0,752},{8,760},{16,0},{24,8},{32,16},{40,24},{48,32},{56,40},{64,... | collective-permute-start | bytes 294920 | tf_op jit(solution)/shard_map/ppermute | solution.py:9
  124.5 9.8 %collective-permute-start.5 = (bf16[96,4,128]{2,1,0:T(4,128)(2,1)S(1)}, bf16[96,4,128]{2,1,0:T(4,128)(2,1)S(1)}, u32[]{:S(2)}, u32[]{:S(2)}) collective-permute-start(bf16[96,4,128]{2,1,0:T(4,128)(2,1)S(1)} %get-tuple-element.14), channel_id=1, source_target_pairs={{0,8},{8,16},{16,24},{24,32},{32,40},{40,48},{48,56},{56,64},{64,7... | collective-permute-start | bytes 294920 | tf_op jit(solution)/shard_map/ppermute | solution.py:9
  126.5 8.4 %collective-permute-start.4 = (bf16[96,4,128]{2,1,0:T(4,128)(2,1)S(1)}, bf16[96,4,128]{2,1,0:T(4,128)(2,1)S(1)}, u32[]{:S(2)}, u32[]{:S(2)}) collective-permute-start(bf16[96,4,128]{2,1,0:T(4,128)(2,1)S(1)} %get-tuple-element.11), channel_id=1, source_target_pairs={{0,760},{8,0},{16,8},{24,16},{32,24},{40,32},{48,40},{56,48},{64,5... | collective-permute-start | bytes 294920 | tf_op jit(solution)/shard_map/ppermute | solution.py:9
  (4 other events, 4.8 us)
Sparse Core Ops, SparseCore 0:
  94.6 468.8 all-reduce.1
where the time goes:
time: 574 us
  waiting for transfers between devices  446 us (78%)
  starting transfers between devices  57.8 us (10%)
  local copies, waits for them, and re-layouts  24.3 us (4%)
  matrix products  22.8 us (4%)
  between operations  14.4 us (3%)
  other arithmetic  8.71 us (2%)
    psum x1, waiting for transfers between devices, shards(): d_weight = lax.psum(local_term, ('dom', 'sub'))  425 us
    ppermute x8, starting transfers between devices, passed_along(): lax.ppermute(array, axis, [(i, (i + by) % devices) for i in range(devices)])  47.7 us
    all_to_all x1, waiting for transfers between devices, shards(): lax.all_to_all(aggregated, 'sub', split_axis=1, concat_axis=0, tiled=True)  12 us
  transfers between devices with their start and end apart: 11, of which 4 were waited for; matrix products, arithmetic and copies ran while one was open for 5% of the time, Pallas kernels for 0%

commit v1 on v0

v1 whole, which is shorter than its diff:
```python
import functools

import jax
import jax.numpy as jnp
from jax import lax
from jax.experimental import pallas as pl
from jax.experimental.pallas import tpu as pltpu
from jax.sharding import PartitionSpec as P

ROWS_Y = 8
CORES = 2
ONES = 16
F32 = jnp.float32
BF16 = jnp.bfloat16
FAR_FIRST = {4: (2, 1, 3, 0), 2: (1, 0)}


def offset_of(position):
    return (position // 2 + 1) * (1 - 2 * (position % 2))


def order_by(keys, attributes, key_count):
    size = keys.shape[1]
    row = lax.broadcasted_iota(jnp.int32, (size, size), 0)
    lane = lax.broadcasted_iota(jnp.int32, (size, size), 1)

    def column(values):
        spread = jnp.broadcast_to(values, (size, size))
        return jnp.sum(jnp.where(row == lane, spread, 0.0), axis=1, keepdims=True)

    keys_column = column(keys)
    same = jnp.broadcast_to(keys, (size, size)) == keys_column
    less = jnp.broadcast_to(keys, (size, size)) < keys_column
    earlier = same & (lane < row)
    rank = jnp.sum(jnp.where(less | earlier, 1.0, 0.0), axis=1, keepdims=True)
    keep = jnp.minimum(jnp.sum(jnp.where(earlier, 1.0, 0.0), axis=1, keepdims=True), 1.0)
    hit = jnp.where(rank == lane.astype(F32), 1.0, 0.0)

    def placed(values):
        return jnp.sum(hit * values, axis=0, keepdims=True)

    wanted = lax.broadcasted_iota(jnp.int32, (size, key_count), 1).astype(F32)
    last = jnp.sum(jnp.where(keys_column <= wanted, 1.0, 0.0), axis=0, keepdims=True) - 1.0
    present = jnp.sum(jnp.where(keys_column == wanted, 1.0, 0.0), axis=0, keepdims=True)
    index_column = lax.broadcasted_iota(jnp.int32, (size, 1), 0).astype(F32)
    return (
        [placed(index_column)]
        + [placed(column(values)) for values in attributes]
        + [placed(keep), jnp.maximum(last, 0.0), jnp.minimum(present, 1.0)]
    )


def plan_kernel(blocks, table_len, list_ref, count_ref, dst_ref, src_ref, out_ref):
    _, offsets, capacity = list_ref.shape
    slots = offsets * capacity
    dst = dst_ref[...].astype(F32)
    src = src_ref[...].astype(F32)
    lane = lax.broadcasted_iota(jnp.int32, (1, slots), 1)
    listed = jnp.zeros((1, slots), jnp.int32)
    live = jnp.zeros((1, slots), jnp.int32)
    for j in range(offsets):
        for k in range(capacity):
            here = lane == j * capacity + k
            listed = jnp.where(here, list_ref[0, j, k], listed)
            live = jnp.where(here & (k < count_ref[0, j]), 1, live)
    owner = jnp.where(live == 1, listed, blocks).astype(F32)
    rows = (
        order_by(dst, [src], blocks)
        + order_by(src, [dst], table_len)
        + [listed.astype(F32)]
        + order_by(owner, [], blocks)
    )
    out_ref[...] = jnp.zeros_like(out_ref)
    for index, values in enumerate(rows):
        out_ref[index : index + 1, : values.shape[1]] = values.astype(jnp.int32)


def kernel(
    cols_x,
    plan,
    feats,
    weight,
    mask,
    cot,
    hidden,
    d_feats,
    d_weight,
    table,
    mask_int,
    mask_half,
    sums,
    w,
    wt,
    cot_v,
    outgoing,
    incoming,
    agg,
    full,
    scales,
    hid,
    d_pre,
    d_agg,
    dw_out,
    dw_own,
    core_in,
    x_out,
    x_in,
    z_out,
    z_in,
    y_all,
    gathered,
    back,
    scaled,
    returning,
    returned,
    slot_sums,
    result,
    local_sem,
    tile_sem,
    perm_sem,
    ret_sem,
    a2a_sem,
    back_sem,
    core_sem,
    x_sem,
    z_sem,
    y_sem,
    gz_sem,
    gx_sem,
    gc_sem,
):
    width, span = feats.shape
    edges, block, _ = mask.shape
    features = weight.shape[0]
    blocks = span // block
    slots = returned.shape[0]
    offsets = perm_sem.shape[1]
    capacity = slots // offsets
    subs = cols_x * CORES
    per_sub = blocks // subs
    half = features // CORES
    xrows = half // cols_x
    doms = lax.axis_size("dom")
    deep = doms // ROWS_Y
    wide = features // 2

    dom, sub = lax.axis_index("dom"), lax.axis_index("sub")
    z, y = dom // ROWS_Y, dom % ROWS_Y
    x, core = sub // CORES, sub % CORES
    sibling = x * CORES + 1 - core

    def tile(index):
        return pl.ds(pl.multiple_of(index * block, block), block)

    def push(src, dst, sems, index, to_dom, to_sub):
        copy = pltpu.make_async_remote_copy(
            src_ref=src,
            dst_ref=dst,
            send_sem=sems.at[0, index],
            recv_sem=sems.at[1, index],
            device_id=(to_dom, to_sub),
            device_id_type=pl.DeviceIdType.MESH,
        )
        copy.start()
        return copy

    def fetch(src, dst, index):
        copy = pltpu.make_async_copy(src, dst, local_sem.at[index])
        copy.start()
        return copy

    in_dom = [lax.rem(dom + offset_of(j) + doms, doms) for j in range(offsets)]
    against = [lax.rem(dom - offset_of(j) + doms, doms) for j in range(offsets)]
    in_sub = [
        (o * CORES + d, lax.rem(x + o, cols_x) * CORES + lax.rem(core + d, CORES))
        for o in FAR_FIRST[cols_x]
        for d in range(CORES)
        if o or d
    ]
    in_x = [(o, lax.rem(x + o, cols_x)) for o in FAR_FIRST[cols_x] if o]
    in_z = [(o, lax.rem(z + o, deep)) for o in range(1, deep)]
    in_y = [(o, lax.rem(y + o, ROWS_Y)) for o in range(1, ROWS_Y)]

    barrier = pltpu.get_barrier_semaphore()
    partners = (
        [(d, sub) for d in in_dom]
        + [(dom, s) for _, s in in_sub]
        + [(other * ROWS_Y + y, sub) for _, other in in_z]
        + [(z * ROWS_Y + other, sub) for _, other in in_y]
    )
    for partner in partners:
        pl.semaphore_signal(
            barrier, inc=1, device_id=partner, device_id_type=pl.DeviceIdType.MESH
        )

    def own_tile(b):
        return pltpu.make_async_copy(feats.at[:, tile(b)], table.at[b, :width], tile_sem.at[b])

    def start_tile(b, carry):
        own_tile(b).start()
        return carry

    lax.fori_loop(0, blocks, start_tile, 0)
    quarter = edges // 4
    mask_in = [
        fetch(mask.at[pl.ds(i * quarter, quarter)], mask_int.at[pl.ds(i * quarter, quarter)], 1 + i)
        for i in range(4)
    ]
    w_in = fetch(weight, w, 5)
    cot_in = fetch(cot, cot_v, 6)

    def ones_below(t, carry):
        table[t, width:, :] = jnp.ones((ONES, block), BF16)
        return carry

    lax.fori_loop(0, blocks + slots, ones_below, 0)

    def wait_tile(b, carry):
        own_tile(b).wait()
        return carry

    lax.fori_loop(0, blocks, wait_tile, 0)
    for slot in range(slots):
        outgoing[slot] = table[plan[10, slot]][:width]
    pl.semaphore_wait(barrier, len(partners))

    sent = [
        push(
            outgoing.at[pl.ds(j * capacity, capacity)],
            incoming.at[pl.ds(j * capacity, capacity)],
            perm_sem,
            j,
            in_dom[j],
            sub,
        )
        for j in range(offsets)
    ]
    for i in range(4):
        mask_in[i].wait()

        def halve(e, carry):
            mask_half[e] = mask_int[e].astype(F32).astype(BF16)
            return carry

        lax.fori_loop(i * quarter, (i + 1) * quarter, halve, 0, unroll=2)
    w_in.wait()
    strip = features // 4
    for i in range(4):
        wt[:, i * strip : (i + 1) * strip] = w[i * strip : (i + 1) * strip, :].T
    for copy in sent:
        copy.wait_recv()
    table[blocks:, :width, :] = incoming[...]

    def forward(q, running):
        product = lax.dot_general(
            table[plan[1, q]],
            mask_half[plan[0, q]],
            (((1,), (1,)), ((), ())),
            preferred_element_type=F32,
        )
        running = running * plan[2, q].astype(F32) + product
        sums[q] = running
        return running

    lax.fori_loop(0, edges, forward, jnp.zeros((width + ONES, block), F32), unroll=4)

    def aggregate(s):
        def one(i, carry):
            b = s * per_sub + i
            total = sums[plan[3, b]] * plan[4, b].astype(F32)
            scale = lax.rsqrt(1.0 + total[width : width + 1])
            scales[b] = jnp.broadcast_to(scale, (8, block))
            own = table[b, :width, :].astype(F32)
            agg[s, :, tile(i)] = ((own + total[:width]) * scale).astype(BF16)
            return carry

        lax.fori_loop(0, per_sub, one, 0)

    own_rows = pl.ds(pl.multiple_of(sub * width, width), width)
    across = []
    for index, s in in_sub:
        aggregate(s)
        across.append(push(agg.at[s], full.at[own_rows], a2a_sem, index, dom, s))
    aggregate(sub)
    full[own_rows, :] = agg[sub]
    cot_in.wait()
    for copy in across:
        copy.wait_recv()

    def transform(i, carry):
        rows = pl.ds(pl.multiple_of(i * strip, strip), strip)
        pre = jnp.dot(w[rows, :], full[...], preferred_element_type=F32)
        gate = 1.0 / (1.0 + jnp.exp(-pre))
        hid[rows, :] = (pre * gate).astype(BF16)
        d_pre[rows, :] = (
            cot_v[rows, :].astype(F32) * gate * (1.0 + pre * (1.0 - gate))
        ).astype(BF16)
        return carry

    lax.fori_loop(0, 4, transform, 0)
    hid_out = fetch(hid, hidden, 7)

    def term(i):
        rows = pl.ds(pl.multiple_of(i * strip, strip), strip)
        return lax.dot_general(
            d_pre[rows, :], full[...], (((1,), (1,)), ((), ())), preferred_element_type=F32
        )

    def local_rows(i):
        return pl.ds(pl.multiple_of(i * strip, strip), strip)

    def for_sibling(i, carry):
        dw_out[local_rows(i), :] = term((1 - core) * 2 + i).astype(BF16)
        return carry

    lax.fori_loop(0, 2, for_sibling, 0)
    to_core = push(dw_out, core_in, core_sem, 0, dom, sibling)

    def for_self(i, carry):
        dw_own[local_rows(i), :] = term(core * 2 + i)
        return carry

    lax.fori_loop(0, 2, for_self, 0)
    pair = CORES * width

    def gradient(i, carry):
        rows = pl.ds(pl.multiple_of(i * pair, pair), pair)
        product = jnp.dot(wt[rows, :], d_pre[...], preferred_element_type=F32).astype(BF16)
        for k in range(per_sub):
            d_agg[k, rows, :] = product[:, k * block : (k + 1) * block]
        return carry

    lax.fori_loop(0, cols_x, gradient, 0)

    def x_rows(i):
        return pl.ds(pl.multiple_of(i * xrows, xrows), xrows)

    to_core.wait_recv()

    def add_core(i, carry):
        total = dw_own[x_rows(i), :] + core_in[x_rows(i), :].astype(F32)
        dw_own[x_rows(i), :] = total
        x_out[x_rows(i), :] = total.astype(BF16)
        return carry

    lax.fori_loop(0, cols_x, add_core, 0)
    to_x = [
        push(x_out.at[x_rows(other)], x_in.at[o - 1], x_sem, o, dom, other * CORES + core)
        for o, other in in_x
    ]
    own_blocks = pl.ds(sub * per_sub, per_sub)
    backward = [
        push(
            d_agg.at[:, pl.ds(pl.multiple_of(s * width, width), width)],
            back.at[own_blocks],
            back_sem,
            index,
            dom,
            s,
        )
        for index, s in in_sub
    ]
    back[own_blocks] = d_agg[:, own_rows, :]

    def z_part(i):
        return (
            pl.ds(pl.multiple_of((i // 2) * 16, 16), 16),
            pl.ds(pl.multiple_of((i % 2) * wide, wide), wide),
        )

    for copy in to_x:
        copy.wait_recv()
    total = dw_own[x_rows(x), :]
    for o in range(cols_x - 1):
        total = total + x_in[o].astype(F32)
    dw_own[:xrows, :] = total
    z_out[...] = total.astype(BF16)
    to_z = [
        push(z_out.at[z_part(other)], z_in.at[o - 1], z_sem, o, other * ROWS_Y + y, sub)
        for o, other in in_z
    ]
    for copy in backward:
        copy.wait_recv()

    def rescale(b, carry):
        scaled[b] = (back[b].astype(F32) * scales[b][:1]).astype(BF16)
        return carry

    lax.fori_loop(0, blocks, rescale, 0, unroll=2)
    for copy in to_z:
        copy.wait_recv()
    rows, columns = z_part(z)
    total = dw_own[rows, columns]
    for o in range(deep - 1):
        total = total + z_in[o].astype(F32)
    y_all[y] = total.astype(BF16)
    to_y = [
        push(y_all.at[y], y_all.at[y], y_sem, o, z * ROWS_Y + other, sub) for o, other in in_y
    ]

    def backward_edge(q, running):
        product = jnp.dot(
            scaled[plan[6, q]], mask_half[plan[5, q]], preferred_element_type=F32
        )
        running = running * plan[7, q].astype(F32) + product
        sums[q, :width, :] = running
        return running

    lax.fori_loop(0, edges, backward_edge, jnp.zeros((width, block), F32), unroll=4)
    home = []
    for j in range(offsets):
        for k in range(capacity):
            t = blocks + j * capacity + k
            returning[j * capacity + k] = (
                sums[plan[8, t]][:width] * plan[9, t].astype(F32)
            ).astype(BF16)
        home.append(
            push(
                returning.at[pl.ds(j * capacity, capacity)],
                returned.at[pl.ds(j * capacity, capacity)],
                ret_sem,
                j,
                against[j],
                sub,
            )
        )
    for copy in to_y:
        copy.wait_recv()
    for copy in to_y:
        copy.wait_send()
    total = y_all[0].astype(F32)
    for other in range(1, ROWS_Y):
        total = total + y_all[other].astype(F32)

    def x_strip(of_core, of_x):
        return pl.ds(pl.multiple_of(of_core * half + of_x * xrows, xrows), xrows)

    mine = (
        pl.ds(pl.multiple_of(core * half + x * xrows + (z // 2) * 16, 16), 16),
        pl.ds(pl.multiple_of((z % 2) * wide, wide), wide),
    )
    gathered[mine] = total.astype(BF16)
    over_z = [
        push(gathered.at[mine], gathered.at[mine], gz_sem, o, other * ROWS_Y + y, sub)
        for o, other in in_z
    ]
    for copy in over_z:
        copy.wait_recv()
    strip_x = gathered.at[x_strip(core, x)]
    over_x = [
        push(strip_x, strip_x, gx_sem, o, dom, other * CORES + core) for o, other in in_x
    ]
    over_core = [push(strip_x, strip_x, gc_sem, 0, dom, sibling)]
    for copy in home:
        copy.wait_recv()

    def add_slot(i, running):
        running = running * plan[12, i].astype(F32) + returned[plan[11, i]].astype(F32)
        slot_sums[i] = running
        return running

    lax.fori_loop(0, slots, add_slot, jnp.zeros((width, block), F32))

    def finish(b, carry):
        result[:, tile(b)] = (
            scaled[b].astype(F32)
            + sums[plan[8, b]][:width] * plan[9, b].astype(F32)
            + slot_sums[plan[13, b]] * plan[14, b].astype(F32)
        ).astype(BF16)
        return carry

    lax.fori_loop(0, blocks, finish, 0, unroll=2)
    d_feats_out = fetch(result, d_feats, 8)
    for (o, _), copy in zip(in_x, over_x):
        copy.wait_recv()
        arrived = gathered.at[x_strip(core, lax.rem(x - o + cols_x, cols_x))]
        over_core.append(push(arrived, arrived, gc_sem, o, dom, sibling))
    for copy in over_core:
        copy.wait_recv()
    d_weight_out = fetch(gathered, d_weight, 9)
    for copy in (
        sent + across + [to_core] + to_x + backward + to_z + home + over_z + over_x + over_core
    ):
        copy.wait_send()
    hid_out.wait()
    d_feats_out.wait()
    d_weight_out.wait()


def shards(cols_x, feats, weight, edge_dst, edge_src, edge_mask, send_list, send_count, cotangent):
    width, span = feats.shape
    _, edges, block, _ = edge_mask.shape
    features = weight.shape[0]
    blocks = span // block
    _, offsets, capacity = send_list.shape
    slots = offsets * capacity
    table_len = blocks + slots
    subs = cols_x * CORES
    labels = span // subs
    half = features // CORES
    xrows = half // cols_x
    deep = lax.axis_size("dom") // ROWS_Y
    vmem, smem, anywhere = (
        pl.BlockSpec(memory_space=space) for space in (pltpu.VMEM, pltpu.SMEM, pl.ANY)
    )
    plan = pl.pallas_call(
        functools.partial(plan_kernel, blocks, table_len),
        out_shape=jax.ShapeDtypeStruct((16, 128), jnp.int32),
        in_specs=[smem, smem, vmem, vmem],
        out_specs=vmem,
    )(send_list, send_count, edge_dst, edge_src)
    dma = pltpu.SemaphoreType.DMA
    hidden, d_feats, d_weight = pl.pallas_call(
        functools.partial(kernel, cols_x),
        out_shape=(
            jax.ShapeDtypeStruct((features, labels), BF16),
            jax.ShapeDtypeStruct((width, span), BF16),
            jax.ShapeDtypeStruct((features, features), BF16),
        ),
        in_specs=[smem] + [anywhere] * 4,
        out_specs=(anywhere,) * 3,
        scratch_shapes=[
            pltpu.VMEM((table_len, width + ONES, block), BF16),
            pltpu.VMEM((edges, block, block), jnp.int32),
            pltpu.VMEM((edges, block, block), BF16),
            pltpu.VMEM((edges, width + ONES, block), F32),
            pltpu.VMEM((features, features), BF16),
            pltpu.VMEM((features, features), BF16),
            pltpu.VMEM((features, labels), BF16),
            pltpu.VMEM((slots, width, block), BF16),
            pltpu.VMEM((slots, width, block), BF16),
            pltpu.VMEM((subs, width, labels), BF16),
            pltpu.VMEM((features, labels), BF16),
            pltpu.VMEM((blocks, 8, block), F32),
            pltpu.VMEM((features, labels), BF16),
            pltpu.VMEM((features, labels), BF16),
            pltpu.VMEM((labels // block, features, block), BF16),
            pltpu.VMEM((half, features), BF16),
            pltpu.VMEM((half, features), F32),
            pltpu.VMEM((half, features), BF16),
            pltpu.VMEM((half, features), BF16),
            pltpu.VMEM((cols_x - 1, xrows, features), BF16),
            pltpu.VMEM((xrows, features), BF16),
            pltpu.VMEM((deep - 1, 16, features // 2), BF16),
            pltpu.VMEM((ROWS_Y, 16, features // 2), BF16),
            pltpu.VMEM((features, features), BF16),
            pltpu.VMEM((blocks, width, block), BF16),
            pltpu.VMEM((blocks, width, block), BF16),
            pltpu.VMEM((slots, width, block), BF16),
            pltpu.VMEM((slots, width, block), BF16),
            pltpu.VMEM((slots, width, block), F32),
            pltpu.VMEM((width, span), BF16),
            dma((10,)),
            dma((blocks,)),
            dma((2, offsets)),
            dma((2, offsets)),
            dma((2, subs)),
            dma((2, subs)),
            dma((2, 1)),
            dma((2, cols_x)),
            dma((2, deep)),
            dma((2, ROWS_Y)),
            dma((2, deep)),
            dma((2, cols_x)),
            dma((2, cols_x)),
        ],
        compiler_params=pltpu.CompilerParams(
            collective_id=0, has_side_effects=True, vmem_limit_bytes=48 * 1024 * 1024
        ),
    )(plan, feats, weight, edge_mask[0], cotangent)
    return (hidden, d_feats, d_weight.astype(F32))


def solution(mesh):
    cols_x = mesh.shape["sub"] // CORES
    return jax.shard_map(
        functools.partial(shards, cols_x),
        mesh=mesh,
        in_specs=(
            P("sub", "dom"),
            P(),
            P("dom", None),
            P("dom", None),
            P("dom", None, None, None),
            P("dom", None, None),
            P("dom", None),
            P(None, ("dom", "sub")),
        ),
        out_specs=(P(None, ("dom", "sub")), P("sub", "dom"), P()),
        check_vma=False,
    )
```

time: 574 us -> 98.2 us (0.17)
  waiting for transfers between devices: 446 us -> 0 us
  Pallas kernels: 0 us -> 89.3 us
  starting transfers between devices: 57.8 us -> 0 us
  matrix products: 22.8 us -> 0 us
  local copies, waits for them, and re-layouts: 24.3 us -> 5.99 us
  between operations: 14.4 us -> 0.65 us
  other arithmetic: 8.71 us -> 1.58 us
    psum x1 -> x0, waiting for transfers between devices: 425 us -> none  [shards(): d_weight = lax.psum(local_term, ('dom', 'sub'))]
    pallas_call x0 -> x2, Pallas kernels: none -> 89.3 us  [the longest x1 87.8 us: shards(): pl.pallas_call(functools.partial(kernel, cols_x), out_shape=(jax.ShapeDty...]
    ppermute x8 -> x0, starting transfers between devices: 47.7 us -> none  [passed_along(): lax.ppermute(array, axis, [(i, (i + by) % devices) for i in range(devices)])]
    dot_general x9 -> x0, matrix products: 22.8 us -> none  [the longest x1 4.83 us: shards(): d_table = jnp.einsum('ceq,et->ctq', d_source, source_hot, precision=highest)]
    all_to_all x2 -> x0, waiting for transfers between devices: 19.6 us -> none  [the longest x1 12 us: shards(): lax.all_to_all(aggregated, 'sub', split_axis=1, concat_axis=0, tiled=True)]
    all_to_all x2 -> x0, starting transfers between devices: 10.1 us -> none  [the longest x1 5.81 us: shards(): lax.all_to_all(aggregated, 'sub', split_axis=1, concat_axis=0, tiled=True)]
  transfers between devices with their start and end apart: 11 -> 0, of which waited for: 4 -> 0; matrix products, arithmetic and copies ran while one was open for 5% -> 0% of each run, Pallas kernels for 0% -> 0%
where the time goes in v1:
time: 98.2 us; the launch traced here: 97.6 us
  Pallas kernels  89.3 us (91%)
  local copies, waits for them, and re-layouts  5.99 us (6%)
  other arithmetic  1.58 us (2%)
    pallas_call x1, Pallas kernels, shards(): pl.pallas_call(functools.partial(kernel, cols_x), out_shape=(jax.ShapeDty...  87.8 us
    unnamed x10, local copies, waits for them, and re-layouts  5.99 us

profile of v1, /device:TPU:1, one launch (start us, length us, event | category | flops | bytes accessed | tf_op | source)
XLA Modules:
  0.0 97.6 jit_solution(10792354624992977162)
XLA Ops:
  0.6 1.5 %shard_map.103.plan = s32[16,128]{1,0:T(8,128)} custom-call(s32[1,4,4]{2,1,0:T(4,128)} %list_ref.1, s32[1,4]{1,0:T(1,128)} %count_ref.1, s32[1,64]{1,0:T(1,128)} %dst_ref.1, s32[1,64]{1,0:T(1,128)} %src_ref.1), custom_call_target="tpu_custom_call" | custom-call | tf_op jit(solution)/shard_map/pallas_call | solution.py:506
  2.2 0.0 copy-start
  2.2 1.3 %copy-done = bf16[768,768]{1,0:T(8,128)(2,1)S(1)} copy-done((bf16[768,768]{1,0:T(8,128)(2,1)S(1)}, bf16[768,768]{1,0:T(8,128)(2,1)}, u32[]{:S(2)}) %copy-start) | copy-done | bytes 1179672
  3.4 0.0 copy-start.1
  3.4 1.1 %copy-done.1 = bf16[96,4096]{1,0:T(8,128)(2,1)S(1)} copy-done((bf16[96,4096]{1,0:T(8,128)(2,1)S(1)}, bf16[96,4096]{1,0:T(8,128)(2,1)}, u32[]{:S(2)}) %copy-start.1) | copy-done | bytes 786456
  4.6 0.0 copy-start.2
  4.6 1.1 %copy-done.2 = bf16[768,512]{1,0:T(8,128)(2,1)S(1)} copy-done((bf16[768,512]{1,0:T(8,128)(2,1)S(1)}, bf16[768,512]{1,0:T(8,128)(2,1)}, u32[]{:S(2)}) %copy-start.2) | copy-done | bytes 786456
  5.7 0.0 copy-start.3
  5.7 0.7 copy-done.3
  6.4 87.8 %shard_map.104 = (bf16[768,512]{1,0:T(8,128)(2,1)S(1)}, bf16[96,4096]{1,0:T(8,128)(2,1)S(1)}, bf16[768,768]{1,0:T(8,128)(2,1)S(1)}) custom-call(s32[16,128]{1,0:T(8,128)S(1)} %copy-done.3, bf16[96,4096]{1,0:T(8,128)(2,1)S(1)} %copy-done.1, bf16[768,768]{1,0:T(8,128)(2,1)S(1)} %copy-done, s32[64,128,128]{2,1,0:T(8,128)} %bitcast.1, bf16[768,512]{1,0:T(8,128)(2,1)S(1)} %copy-done.2), custom_call_target="tpu_custom_call" | custom-call | tf_op jit(solution)/shard_map/pallas_call | solution.py:513
  94.2 1.6 %convert_element_type.3 = f32[768,768]{1,0:T(8,128)} convert(bf16[768,768]{1,0:T(8,128)(2,1)S(1)} %get-tuple-element.8) | non-fusion elementwise | flops 589824 | bytes 3538944 | tf_op jit(solution)/shard_map/convert_element_type | solution.py:571
  95.8 0.9 copy.13
  96.7 0.9 copy.14
Async XLA Ops:
  2.2 1.3 %copy-start = (bf16[768,768]{1,0:T(8,128)(2,1)S(1)}, bf16[768,768]{1,0:T(8,128)(2,1)}, u32[]{:S(2)}) copy-start(bf16[768,768]{1,0:T(8,128)(2,1)} %weight.1) | copy-start | bytes 3538948
  3.4 1.1 %copy-start.1 = (bf16[96,4096]{1,0:T(8,128)(2,1)S(1)}, bf16[96,4096]{1,0:T(8,128)(2,1)}, u32[]{:S(2)}) copy-start(bf16[96,4096]{1,0:T(8,128)(2,1)} %feats.1) | copy-start | bytes 2359300
  4.6 1.1 %copy-start.2 = (bf16[768,512]{1,0:T(8,128)(2,1)S(1)}, bf16[768,512]{1,0:T(8,128)(2,1)}, u32[]{:S(2)}) copy-start(bf16[768,512]{1,0:T(8,128)(2,1)} %cot.1) | copy-start | bytes 2359300
  5.7 0.7 copy-start.3

commit v2 on v1

--- a/solution.py
+++ b/solution.py
@@ -10,6 +10,7 @@
 ROWS_Y = 8
 CORES = 2
 ONES = 16
+VMEM_BYTES = 60 * 1024 * 1024
 F32 = jnp.float32
 BF16 = jnp.bfloat16
 FAR_FIRST = {4: (2, 1, 3, 0), 2: (1, 0)}
@@ -108,7 +109,7 @@
     z_out,
     z_in,
     y_all,
-    gathered,
+    summed,
     back,
     scaled,
     returning,
@@ -181,6 +182,15 @@
     in_z = [(o, lax.rem(z + o, deep)) for o in range(1, deep)]
     in_y = [(o, lax.rem(y + o, ROWS_Y)) for o in range(1, ROWS_Y)]
 
+    def own_tile(b):
+        return pltpu.make_async_copy(feats.at[:, tile(b)], table.at[b, :width], tile_sem.at[b])
+
+    def start_tile(b, carry):
+        own_tile(b).start()
+        return carry
+
+    lax.fori_loop(0, blocks, start_tile, 0)
+
     barrier = pltpu.get_barrier_semaphore()
     partners = (
         [(d, sub) for d in in_dom]
@@ -193,14 +203,6 @@
             barrier, inc=1, device_id=partner, device_id_type=pl.DeviceIdType.MESH
         )
 
-    def own_tile(b):
-        return pltpu.make_async_copy(feats.at[:, tile(b)], table.at[b, :width], tile_sem.at[b])
-
-    def start_tile(b, carry):
-        own_tile(b).start()
-        return carry
-
-    lax.fori_loop(0, blocks, start_tile, 0)
     quarter = edges // 4
     mask_in = [
         fetch(mask.at[pl.ds(i * quarter, quarter)], mask_int.at[pl.ds(i * quarter, quarter)], 1 + i)
@@ -287,50 +289,32 @@
     for copy in across:
         copy.wait_recv()
 
-    def transform(i, carry):
-        rows = pl.ds(pl.multiple_of(i * strip, strip), strip)
+    def half_rows(i):
+        return pl.ds(pl.multiple_of(i * half, half), half)
+
+    def transform(i):
+        rows = half_rows(i)
         pre = jnp.dot(w[rows, :], full[...], preferred_element_type=F32)
         gate = 1.0 / (1.0 + jnp.exp(-pre))
         hid[rows, :] = (pre * gate).astype(BF16)
         d_pre[rows, :] = (
             cot_v[rows, :].astype(F32) * gate * (1.0 + pre * (1.0 - gate))
         ).astype(BF16)
-        return carry
-
-    lax.fori_loop(0, 4, transform, 0)
+
+    def term(i):
+        return lax.dot_general(
+            d_pre[half_rows(i), :],
+            full[...],
+            (((1,), (1,)), ((), ())),
+            preferred_element_type=F32,
+        )
+
+    transform(1 - core)
+    dw_out[...] = term(1 - core).astype(BF16)
+    to_core = push(dw_out, core_in, core_sem, 0, dom, sibling)
+    transform(core)
     hid_out = fetch(hid, hidden, 7)
-
-    def term(i):
-        rows = pl.ds(pl.multiple_of(i * strip, strip), strip)
-        return lax.dot_general(
-            d_pre[rows, :], full[...], (((1,), (1,)), ((), ())), preferred_element_type=F32
-        )
-
-    def local_rows(i):
-        return pl.ds(pl.multiple_of(i * strip, strip), strip)
-
-    def for_sibling(i, carry):
-        dw_out[local_rows(i), :] = term((1 - core) * 2 + i).astype(BF16)
-        return carry
-
-    lax.fori_loop(0, 2, for_sibling, 0)
-    to_core = push(dw_out, core_in, core_sem, 0, dom, sibling)
-
-    def for_self(i, carry):
-        dw_own[local_rows(i), :] = term(core * 2 + i)
-        return carry
-
-    lax.fori_loop(0, 2, for_self, 0)
-    pair = CORES * width
-
-    def gradient(i, carry):
-        rows = pl.ds(pl.multiple_of(i * pair, pair), pair)
-        product = jnp.dot(wt[rows, :], d_pre[...], preferred_element_type=F32).astype(BF16)
-        for k in range(per_sub):
-            d_agg[k, rows, :] = product[:, k * block : (k + 1) * block]
-        return carry
-
-    lax.fori_loop(0, cols_x, gradient, 0)
+    dw_own[...] = term(core)
 
     def x_rows(i):
         return pl.ds(pl.multiple_of(i * xrows, xrows), xrows)
@@ -347,6 +331,33 @@
     to_x = [
         push(x_out.at[x_rows(other)], x_in.at[o - 1], x_sem, o, dom, other * CORES + core)
         for o, other in in_x
+    ]
+
+    def gradient(i, carry):
+        rows = half_rows(i)
+        product = jnp.dot(wt[rows, :], d_pre[...], preferred_element_type=F32).astype(BF16)
+        for k in range(per_sub):
+            d_agg[k, rows, :] = product[:, k * block : (k + 1) * block]
+        return carry
+
+    lax.fori_loop(0, CORES, gradient, 0)
+
+    def z_part(i):
+        return (
+            pl.ds(pl.multiple_of((i // 2) * 16, 16), 16),
+            pl.ds(pl.multiple_of((i % 2) * wide, wide), wide),
+        )
+
+    for copy in to_x:
+        copy.wait_recv()
+    total = dw_own[x_rows(x), :]
+    for o in range(cols_x - 1):
+        total = total + x_in[o].astype(F32)
+    dw_own[:xrows, :] = total
+    z_out[...] = total.astype(BF16)
+    to_z = [
+        push(z_out.at[z_part(other)], z_in.at[o - 1], z_sem, o, other * ROWS_Y + y, sub)
+        for o, other in in_z
     ]
     own_blocks = pl.ds(sub * per_sub, per_sub)
     backward = [
@@ -361,32 +372,6 @@
         for index, s in in_sub
     ]
     back[own_blocks] = d_agg[:, own_rows, :]
-
-    def z_part(i):
-        return (
-            pl.ds(pl.multiple_of((i // 2) * 16, 16), 16),
-            pl.ds(pl.multiple_of((i % 2) * wide, wide), wide),
-        )
-
-    for copy in to_x:
-        copy.wait_recv()
-    total = dw_own[x_rows(x), :]
-    for o in range(cols_x - 1):
-        total = total + x_in[o].astype(F32)
-    dw_own[:xrows, :] = total
-    z_out[...] = total.astype(BF16)
-    to_z = [
-        push(z_out.at[z_part(other)], z_in.at[o - 1], z_sem, o, other * ROWS_Y + y, sub)
-        for o, other in in_z
-    ]
-    for copy in backward:
-        copy.wait_recv()
-
-    def rescale(b, carry):
-        scaled[b] = (back[b].astype(F32) * scales[b][:1]).astype(BF16)
-        return carry
-
-    lax.fori_loop(0, blocks, rescale, 0, unroll=2)
     for copy in to_z:
         copy.wait_recv()
     rows, columns = z_part(z)
@@ -397,7 +382,32 @@
     to_y = [
         push(y_all.at[y], y_all.at[y], y_sem, o, z * ROWS_Y + other, sub) for o, other in in_y
     ]
-
+    for copy in to_y:
+        copy.wait_recv()
+    total = y_all[0].astype(F32)
+    for other in range(1, ROWS_Y):
+        total = total + y_all[other].astype(F32)
+    summed[...] = total.astype(BF16)
+
+    def x_strip(of_core, of_x):
+        return pl.ds(pl.multiple_of(of_core * half + of_x * xrows, xrows), xrows)
+
+    mine = (
+        pl.ds(pl.multiple_of(core * half + x * xrows + (z // 2) * 16, 16), 16),
+        pl.ds(pl.multiple_of((z % 2) * wide, wide), wide),
+    )
+    over_z = [
+        push(summed, d_weight.at[mine], gz_sem, o, other * ROWS_Y + y, sub) for o, other in in_z
+    ]
+    own_piece = fetch(summed, d_weight.at[mine], 0)
+    for copy in backward:
+        copy.wait_recv()
+
+    def rescale(b, carry):
+        scaled[b] = (back[b].astype(F32) * scales[b][:1]).astype(BF16)
+        return carry
+
+    lax.fori_loop(0, blocks, rescale, 0, unroll=2)
     def backward_edge(q, running):
         product = jnp.dot(
             scaled[plan[6, q]], mask_half[plan[5, q]], preferred_element_type=F32
@@ -424,29 +434,10 @@
                 sub,
             )
         )
-    for copy in to_y:
-        copy.wait_recv()
-    for copy in to_y:
-        copy.wait_send()
-    total = y_all[0].astype(F32)
-    for other in range(1, ROWS_Y):
-        total = total + y_all[other].astype(F32)
-
-    def x_strip(of_core, of_x):
-        return pl.ds(pl.multiple_of(of_core * half + of_x * xrows, xrows), xrows)
-
-    mine = (
-        pl.ds(pl.multiple_of(core * half + x * xrows + (z // 2) * 16, 16), 16),
-        pl.ds(pl.multiple_of((z % 2) * wide, wide), wide),
-    )
-    gathered[mine] = total.astype(BF16)
-    over_z = [
-        push(gathered.at[mine], gathered.at[mine], gz_sem, o, other * ROWS_Y + y, sub)
-        for o, other in in_z
-    ]
     for copy in over_z:
         copy.wait_recv()
-    strip_x = gathered.at[x_strip(core, x)]
+    own_piece.wait()
+    strip_x = d_weight.at[x_strip(core, x)]
     over_x = [
         push(strip_x, strip_x, gx_sem, o, dom, other * CORES + core) for o, other in in_x
     ]
@@ -473,18 +464,53 @@
     d_feats_out = fetch(result, d_feats, 8)
     for (o, _), copy in zip(in_x, over_x):
         copy.wait_recv()
-        arrived = gathered.at[x_strip(core, lax.rem(x - o + cols_x, cols_x))]
+        arrived = d_weight.at[x_strip(core, lax.rem(x - o + cols_x, cols_x))]
         over_core.append(push(arrived, arrived, gc_sem, o, dom, sibling))
     for copy in over_core:
         copy.wait_recv()
-    d_weight_out = fetch(gathered, d_weight, 9)
     for copy in (
-        sent + across + [to_core] + to_x + backward + to_z + home + over_z + over_x + over_core
+        sent
+        + across
+        + [to_core]
+        + to_x
+        + backward
+        + to_z
+        + to_y
+        + home
+        + over_z
+        + over_x
+        + over_core
     ):
         copy.wait_send()
     hid_out.wait()
     d_feats_out.wait()
-    d_weight_out.wait()
+
+
+def write_kernel(
+    hid, d_feats, d_weight, hid_out, d_feats_out, d_weight_out, narrow, wide, sem, part_sem
+):
+    parts, rows, _ = narrow.shape
+    whole = [
+        pltpu.make_async_copy(hid, hid_out, sem.at[0]),
+        pltpu.make_async_copy(d_feats, d_feats_out, sem.at[1]),
+    ]
+    spans = [pl.ds(i * rows, rows) for i in range(parts)]
+    into = [
+        pltpu.make_async_copy(d_weight.at[spans[i]], narrow.at[i], part_sem.at[0, i])
+        for i in range(parts)
+    ]
+    out_of = [
+        pltpu.make_async_copy(wide.at[i], d_weight_out.at[spans[i]], part_sem.at[1, i])
+        for i in range(parts)
+    ]
+    for copy in into + whole:
+        copy.start()
+    for i in range(parts):
+        into[i].wait()
+        wide[i] = narrow[i].astype(F32)
+        out_of[i].start()
+    for copy in out_of + whole:
+        copy.wait()
 
 
 def shards(cols_x, feats, weight, edge_dst, edge_src, edge_mask, send_list, send_count, cotangent):
@@ -500,14 +526,15 @@
     half = features // CORES
     xrows = half // cols_x
     deep = lax.axis_size("dom") // ROWS_Y
-    vmem, smem, anywhere = (
-        pl.BlockSpec(memory_space=space) for space in (pltpu.VMEM, pltpu.SMEM, pl.ANY)
+    vmem, smem, hbm, anywhere = (
+        pl.BlockSpec(memory_space=space) for space in (pltpu.VMEM, pltpu.SMEM, pltpu.HBM, pl.ANY)
     )
     plan = pl.pallas_call(
         functools.partial(plan_kernel, blocks, table_len),
         out_shape=jax.ShapeDtypeStruct((16, 128), jnp.int32),
         in_specs=[smem, smem, vmem, vmem],
         out_specs=vmem,
+        compiler_params=pltpu.CompilerParams(vmem_limit_bytes=VMEM_BYTES),
     )(send_list, send_count, edge_dst, edge_src)
     dma = pltpu.SemaphoreType.DMA
     hidden, d_feats, d_weight = pl.pallas_call(
@@ -517,7 +544,7 @@
             jax.ShapeDtypeStruct((width, span), BF16),
             jax.ShapeDtypeStruct((features, features), BF16),
         ),
-        in_specs=[smem] + [anywhere] * 4,
+        in_specs=[smem] + [hbm] * 4,
         out_specs=(anywhere,) * 3,
         scratch_shapes=[
             pltpu.VMEM((table_len, width + ONES, block), BF16),
@@ -543,7 +570,7 @@
             pltpu.VMEM((xrows, features), BF16),
             pltpu.VMEM((deep - 1, 16, features // 2), BF16),
             pltpu.VMEM((ROWS_Y, 16, features // 2), BF16),
-            pltpu.VMEM((features, features), BF16),
+            pltpu.VMEM((16, features // 2), BF16),
             pltpu.VMEM((blocks, width, block), BF16),
             pltpu.VMEM((blocks, width, block), BF16),
             pltpu.VMEM((slots, width, block), BF16),
@@ -565,10 +592,26 @@
             dma((2, cols_x)),
         ],
         compiler_params=pltpu.CompilerParams(
-            collective_id=0, has_side_effects=True, vmem_limit_bytes=48 * 1024 * 1024
+            collective_id=0, has_side_effects=True, vmem_limit_bytes=VMEM_BYTES
         ),
     )(plan, feats, weight, edge_mask[0], cotangent)
-    return (hidden, d_feats, d_weight.astype(F32))
+    return pl.pallas_call(
+        write_kernel,
+        out_shape=(
+            jax.ShapeDtypeStruct((features, labels), BF16),
+            jax.ShapeDtypeStruct((width, span), BF16),
+            jax.ShapeDtypeStruct((features, features), F32),
+        ),
+        in_specs=[anywhere] * 3,
+        out_specs=(hbm,) * 3,
+        scratch_shapes=[
+            pltpu.VMEM((4, features // 4, features), BF16),
+            pltpu.VMEM((4, features // 4, features), F32),
+            dma((2,)),
+            dma((2, 4)),
+        ],
+        compiler_params=pltpu.CompilerParams(vmem_limit_bytes=VMEM_BYTES),
+    )(hidden, d_feats, d_weight)
 
 
 def solution(mesh):

time: 98.2 us -> 137 us (1.40)
  Pallas kernels: 89.3 us -> 137 us
  local copies, waits for them, and re-layouts: 5.99 us -> 0 us
  other arithmetic: 1.58 us -> 0 us
    pallas_call x0 -> x1, Pallas kernels: none -> 48.8 us  [shards(): pl.pallas_call(write_kernel, out_shape=(jax.ShapeDtypeStruct((features, l...]
    unnamed x10 -> x0, local copies, waits for them, and re-layouts: 5.99 us -> none
    pallas_call x1, Pallas kernels: 87.8 us -> 86.2 us  [shards(): pl.pallas_call(functools.partial(kernel, cols_x), out_shape=(jax.ShapeDty...]
    convert_element_type x1 -> x0, other arithmetic: 1.58 us -> none  [shards(): return (hidden, d_feats, d_weight.astype(F32))]
where the time goes in v2:
time: 137 us
  Pallas kernels  137 us (100%)
    pallas_call x1, Pallas kernels, shards(): pl.pallas_call(functools.partial(kernel, cols_x), out_shape=(jax.ShapeDty...  86.2 us
    pallas_call x1, Pallas kernels, shards(): pl.pallas_call(write_kernel, out_shape=(jax.ShapeDtypeStruct((features, l...  48.8 us

profile of v2, /device:TPU:1, one launch (start us, length us, event | category | flops | bytes accessed | tf_op | source)
XLA Modules:
  0.0 137.2 jit_solution(7422132943068222098)
XLA Ops:
  0.6 1.5 %shard_map.103.plan = s32[16,128]{1,0:T(8,128)} custom-call(s32[1,4,4]{2,1,0:T(4,128)} %list_ref.1, s32[1,4]{1,0:T(1,128)} %count_ref.1, s32[1,64]{1,0:T(1,128)} %dst_ref.1, s32[1,64]{1,0:T(1,128)} %src_ref.1), custom_call_target="tpu_custom_call" | custom-call | tf_op jit(solution)/shard_map/pallas_call | solution.py:532
  2.2 86.2 %shard_map.104 = (bf16[768,512]{1,0:T(8,128)(2,1)}, bf16[96,4096]{1,0:T(8,128)(2,1)}, bf16[768,768]{1,0:T(8,128)(2,1)}) custom-call(s32[16,128]{1,0:T(8,128)} %shard_map.103.plan, bf16[96,4096]{1,0:T(8,128)(2,1)} %feats.1, bf16[768,768]{1,0:T(8,128)(2,1)} %weight.1, s32[64,128,128]{2,1,0:T(8,128)} %bitcast.1, bf16[768,512]{1,0:T(8,128)(2,1)} %cot.1), custom_call_target="tpu_custom_call" | custom-call | tf_op jit(solution)/shard_map/pallas_call | solution.py:540
  88.3 48.8 %shard_map.105 = (bf16[768,512]{1,0:T(8,128)(2,1)}, bf16[96,4096]{1,0:T(8,128)(2,1)}, f32[768,768]{1,0:T(8,128)}) custom-call(bf16[768,512]{1,0:T(8,128)(2,1)} %get-tuple-element.6.hid, bf16[96,4096]{1,0:T(8,128)(2,1)} %get-tuple-element.7.d_feats, bf16[768,768]{1,0:T(8,128)(2,1)} %get-tuple-element.8.d_weight), custom_call_target="tpu_custom_call" | custom-call | tf_op jit(solution)/shard_map/pallas_call | solution.py:598

commit v3 on v2

--- a/solution.py
+++ b/solution.py
@@ -10,6 +10,8 @@
 ROWS_Y = 8
 CORES = 2
 ONES = 16
+TALL = 16
+SECOND_PAIRS = 4
 VMEM_BYTES = 60 * 1024 * 1024
 F32 = jnp.float32
 BF16 = jnp.bfloat16
@@ -104,12 +106,20 @@
     dw_out,
     dw_own,
     core_in,
-    x_out,
-    x_in,
-    z_out,
-    z_in,
-    y_all,
-    summed,
+    half_out,
+    y1_in,
+    z1_in,
+    first,
+    second,
+    z2_out,
+    z2_in,
+    x2_out,
+    x2_in,
+    x3_all,
+    y3_all,
+    line,
+    square,
+    gathered,
     back,
     scaled,
     returning,
@@ -123,11 +133,17 @@
     a2a_sem,
     back_sem,
     core_sem,
-    x_sem,
-    z_sem,
-    y_sem,
-    gz_sem,
-    gx_sem,
+    y1_sem,
+    z1_sem,
+    x2_sem,
+    z2_sem,
+    x3_sem,
+    y3_sem,
+    x4_sem,
+    z4_sem,
+    y5_sem,
+    z5_sem,
+    x6_sem,
     gc_sem,
 ):
     width, span = feats.shape
@@ -140,10 +156,11 @@
     subs = cols_x * CORES
     per_sub = blocks // subs
     half = features // CORES
-    xrows = half // cols_x
     doms = lax.axis_size("dom")
     deep = doms // ROWS_Y
     wide = features // 2
+    row_z, across_z = deep // 2, deep // 4
+    lanes = features // row_z
 
     dom, sub = lax.axis_index("dom"), lax.axis_index("sub")
     z, y = dom // ROWS_Y, dom % ROWS_Y
@@ -314,24 +331,6 @@
     to_core = push(dw_out, core_in, core_sem, 0, dom, sibling)
     transform(core)
     hid_out = fetch(hid, hidden, 7)
-    dw_own[...] = term(core)
-
-    def x_rows(i):
-        return pl.ds(pl.multiple_of(i * xrows, xrows), xrows)
-
-    to_core.wait_recv()
-
-    def add_core(i, carry):
-        total = dw_own[x_rows(i), :] + core_in[x_rows(i), :].astype(F32)
-        dw_own[x_rows(i), :] = total
-        x_out[x_rows(i), :] = total.astype(BF16)
-        return carry
-
-    lax.fori_loop(0, cols_x, add_core, 0)
-    to_x = [
-        push(x_out.at[x_rows(other)], x_in.at[o - 1], x_sem, o, dom, other * CORES + core)
-        for o, other in in_x
-    ]
 
     def gradient(i, carry):
         rows = half_rows(i)
@@ -341,24 +340,6 @@
         return carry
 
     lax.fori_loop(0, CORES, gradient, 0)
-
-    def z_part(i):
-        return (
-            pl.ds(pl.multiple_of((i // 2) * 16, 16), 16),
-            pl.ds(pl.multiple_of((i % 2) * wide, wide), wide),
-        )
-
-    for copy in to_x:
-        copy.wait_recv()
-    total = dw_own[x_rows(x), :]
-    for o in range(cols_x - 1):
-        total = total + x_in[o].astype(F32)
-    dw_own[:xrows, :] = total
-    z_out[...] = total.astype(BF16)
-    to_z = [
-        push(z_out.at[z_part(other)], z_in.at[o - 1], z_sem, o, other * ROWS_Y + y, sub)
-        for o, other in in_z
-    ]
     own_blocks = pl.ds(sub * per_sub, per_sub)
     backward = [
         push(
@@ -372,51 +353,108 @@
         for index, s in in_sub
     ]
     back[own_blocks] = d_agg[:, own_rows, :]
-    for copy in to_z:
-        copy.wait_recv()
-    rows, columns = z_part(z)
-    total = dw_own[rows, columns]
+    dw_own[...] = term(core)
+    to_core.wait_recv()
+
+    def add_core(i, carry):
+        rows = pl.ds(pl.multiple_of(i * 2 * TALL, 2 * TALL), 2 * TALL)
+        total = dw_own[rows, :] + core_in[rows, :].astype(F32)
+        dw_own[rows, :] = total
+        half_out[rows, :] = total.astype(BF16)
+        return carry
+
+    lax.fori_loop(0, half // (2 * TALL), add_core, 0)
+
+    def first_part(i):
+        return pl.ds(pl.multiple_of(i * 2 * TALL, 2 * TALL), 2 * TALL), slice(None)
+
+    def second_part(i):
+        return (
+            pl.ds(pl.multiple_of(ROWS_Y * 2 * TALL + (i // across_z) * 2 * TALL, 2 * TALL), 2 * TALL),
+            pl.ds(pl.multiple_of((i % across_z) * 2 * lanes, 2 * lanes), 2 * lanes),
+        )
+
+    def one_tile(i, in_row):
+        return (
+            i // in_row,
+            slice(None),
+            pl.ds(pl.multiple_of((i % in_row) * lanes, lanes), lanes),
+        )
+
+    def tall_tile(i, in_row):
+        return (
+            pl.ds(pl.multiple_of((i // in_row) * TALL, TALL), TALL),
+            pl.ds(pl.multiple_of((i % in_row) * lanes, lanes), lanes),
+        )
+
+    def over_z(src_of, dst_of, sems):
+        return [
+            push(src_of(other), dst_of(o), sems, o, other * ROWS_Y + y, sub) for o, other in in_z
+        ]
+
+    def over_y(src_of, dst_of, sems):
+        return [
+            push(src_of(other), dst_of(o), sems, o, z * ROWS_Y + other, sub) for o, other in in_y
+        ]
+
+    def over_x(src_of, dst_of, sems):
+        return [
+            push(src_of(other), dst_of(o), sems, o, dom, other * CORES + core)
+            for o, other in in_x
+        ]
+
+    def arrive(copies):
+        for copy in copies:
+            copy.wait_recv()
+
+    y1 = over_y(lambda i: half_out.at[first_part(i)], lambda o: y1_in.at[o - 1], y1_sem)
+    z1 = over_z(lambda i: half_out.at[second_part(i)], lambda o: z1_in.at[o - 1], z1_sem)
+    arrive(z1)
+    total = dw_own[second_part(z)]
     for o in range(deep - 1):
-        total = total + z_in[o].astype(F32)
-    y_all[y] = total.astype(BF16)
-    to_y = [
-        push(y_all.at[y], y_all.at[y], y_sem, o, z * ROWS_Y + other, sub) for o, other in in_y
-    ]
-    for copy in to_y:
-        copy.wait_recv()
-    total = y_all[0].astype(F32)
-    for other in range(1, ROWS_Y):
-        total = total + y_all[other].astype(F32)
-    summed[...] = total.astype(BF16)
-
-    def x_strip(of_core, of_x):
-        return pl.ds(pl.multiple_of(of_core * half + of_x * xrows, xrows), xrows)
-
-    mine = (
-        pl.ds(pl.multiple_of(core * half + x * xrows + (z // 2) * 16, 16), 16),
-        pl.ds(pl.multiple_of((z % 2) * wide, wide), wide),
-    )
-    over_z = [
-        push(summed, d_weight.at[mine], gz_sem, o, other * ROWS_Y + y, sub) for o, other in in_z
-    ]
-    own_piece = fetch(summed, d_weight.at[mine], 0)
-    for copy in backward:
-        copy.wait_recv()
+        total = total + z1_in[o].astype(F32)
+    second[...] = total
+    for i in range(2):
+        x2_out[i] = total[i * TALL : (i + 1) * TALL].astype(BF16)
+    x2 = over_x(lambda i: x2_out.at[one_tile(i, 2)], lambda o: x2_in.at[o - 1], x2_sem)
+    arrive(y1)
+    total = dw_own[first_part(y)]
+    for o in range(ROWS_Y - 1):
+        total = total + y1_in[o].astype(F32)
+    first[...] = total
+    for i in range(2):
+        z2_out[i] = total[i * TALL : (i + 1) * TALL].astype(BF16)
+    z2 = over_z(lambda i: z2_out.at[one_tile(i, row_z)], lambda o: z2_in.at[o - 1], z2_sem)
+    arrive(backward)
 
     def rescale(b, carry):
         scaled[b] = (back[b].astype(F32) * scales[b][:1]).astype(BF16)
         return carry
 
     lax.fori_loop(0, blocks, rescale, 0, unroll=2)
+
     def backward_edge(q, running):
-        product = jnp.dot(
-            scaled[plan[6, q]], mask_half[plan[5, q]], preferred_element_type=F32
-        )
+        product = jnp.dot(scaled[plan[6, q]], mask_half[plan[5, q]], preferred_element_type=F32)
         running = running * plan[7, q].astype(F32) + product
         sums[q, :width, :] = running
         return running
 
-    lax.fori_loop(0, edges, backward_edge, jnp.zeros((width, block), F32), unroll=4)
+    running = lax.fori_loop(
+        0, edges // 2, backward_edge, jnp.zeros((width, block), F32), unroll=4
+    )
+    arrive(x2)
+    total = second[tall_tile(x, 2)]
+    for o in range(cols_x - 1):
+        total = total + x2_in[o].astype(F32)
+    y3_all[y] = total.astype(BF16)
+    y3 = over_y(lambda i: y3_all.at[y], lambda o: y3_all.at[y], y3_sem)
+    arrive(z2)
+    total = first[tall_tile(z, row_z)]
+    for o in range(deep - 1):
+        total = total + z2_in[o].astype(F32)
+    x3_all[x] = total.astype(BF16)
+    x3 = over_x(lambda i: x3_all.at[x], lambda o: x3_all.at[x], x3_sem)
+    lax.fori_loop(edges // 2, edges, backward_edge, running, unroll=4)
     home = []
     for j in range(offsets):
         for k in range(capacity):
@@ -434,16 +472,50 @@
                 sub,
             )
         )
-    for copy in over_z:
-        copy.wait_recv()
-    own_piece.wait()
-    strip_x = d_weight.at[x_strip(core, x)]
-    over_x = [
-        push(strip_x, strip_x, gx_sem, o, dom, other * CORES + core) for o, other in in_x
+    arrive(x3)
+    total = x3_all[0].astype(F32)
+    for other in range(1, cols_x):
+        total = total + x3_all[other].astype(F32)
+    mine = one_tile(z, row_z)
+    line[mine] = total.astype(BF16)
+    z4 = over_z(lambda i: line.at[mine], lambda o: line.at[mine], z4_sem)
+    arrive(y3)
+    total = y3_all[0].astype(F32)
+    for other in range(1, ROWS_Y):
+        total = total + y3_all[other].astype(F32)
+    own_tile_x = one_tile(x, 2)
+    square[own_tile_x] = total.astype(BF16)
+    x4 = over_x(lambda i: square.at[own_tile_x], lambda o: square.at[own_tile_x], x4_sem)
+    quarter_of = [
+        (i // 2, slice(None), pl.ds(pl.multiple_of((i % 2) * wide, wide), wide))
+        for i in (x, *(lax.rem(x - o + cols_x, cols_x) for o, _ in in_x))
     ]
-    over_core = [push(strip_x, strip_x, gc_sem, 0, dom, sibling)]
-    for copy in home:
-        copy.wait_recv()
+    arrive(x4)
+    square_at = (
+        core,
+        ROWS_Y + z // across_z,
+        slice(None),
+        slice(None),
+        pl.ds(pl.multiple_of((z % across_z) * 2 * lanes, 2 * lanes), 2 * lanes),
+    )
+    gathered[square_at] = square[...]
+    z5 = over_z(lambda i: square, lambda o: gathered.at[square_at], z5_sem)
+    arrive(z4)
+    own_quarter = quarter_of[0]
+    gathered[(core, y) + own_quarter] = line[own_quarter]
+    y5 = over_y(
+        lambda i: line.at[own_quarter],
+        lambda o: gathered.at[(core, y) + own_quarter],
+        y5_sem,
+    )
+
+    def all_y(quarter):
+        return gathered.at[(core, pl.ds(0, ROWS_Y)) + quarter]
+
+    arrive(y5)
+    x6 = over_x(lambda i: all_y(own_quarter), lambda o: all_y(own_quarter), x6_sem)
+    to_sibling = [push(all_y(own_quarter), all_y(own_quarter), gc_sem, 0, dom, sibling)]
+    arrive(home)
 
     def add_slot(i, running):
         running = running * plan[12, i].astype(F32) + returned[plan[11, i]].astype(F32)
@@ -462,54 +534,57 @@
 
     lax.fori_loop(0, blocks, finish, 0, unroll=2)
     d_feats_out = fetch(result, d_feats, 8)
-    for (o, _), copy in zip(in_x, over_x):
+    arrive(z5)
+    last_rows = gathered.at[core, pl.ds(ROWS_Y, SECOND_PAIRS)]
+    to_sibling.append(push(last_rows, last_rows, gc_sem, cols_x, dom, sibling))
+    for (o, _), copy, quarter in zip(in_x, x6, quarter_of[1:]):
         copy.wait_recv()
-        arrived = d_weight.at[x_strip(core, lax.rem(x - o + cols_x, cols_x))]
-        over_core.append(push(arrived, arrived, gc_sem, o, dom, sibling))
-    for copy in over_core:
-        copy.wait_recv()
-    for copy in (
-        sent
-        + across
-        + [to_core]
-        + to_x
-        + backward
-        + to_z
-        + to_y
-        + home
-        + over_z
-        + over_x
-        + over_core
+        to_sibling.append(push(all_y(quarter), all_y(quarter), gc_sem, o, dom, sibling))
+    arrive(to_sibling)
+    d_weight_out = fetch(gathered, d_weight, 9)
+    for copies in (
+        sent, across, [to_core], backward, y1, z1, x2, z2, x3, y3, home, x4, z4, y5, z5, x6, to_sibling
     ):
-        copy.wait_send()
+        for copy in copies:
+            copy.wait_send()
     hid_out.wait()
     d_feats_out.wait()
+    d_weight_out.wait()
 
 
 def write_kernel(
-    hid, d_feats, d_weight, hid_out, d_feats_out, d_weight_out, narrow, wide, sem, part_sem
+    hid, d_feats, d_weight, hid_out, d_feats_out, d_weight_out, hid_v, d_feats_v, narrow, wide, sem
 ):
-    parts, rows, _ = narrow.shape
-    whole = [
-        pltpu.make_async_copy(hid, hid_out, sem.at[0]),
-        pltpu.make_async_copy(d_feats, d_feats_out, sem.at[1]),
-    ]
-    spans = [pl.ds(i * rows, rows) for i in range(parts)]
-    into = [
-        pltpu.make_async_copy(d_weight.at[spans[i]], narrow.at[i], part_sem.at[0, i])
-        for i in range(parts)
-    ]
-    out_of = [
-        pltpu.make_async_copy(wide.at[i], d_weight_out.at[spans[i]], part_sem.at[1, i])
-        for i in range(parts)
-    ]
-    for copy in into + whole:
+    parts, pairs, _, _, features = narrow.shape
+    per_core = d_weight.shape[1] // pairs
+    rows = features // parts
+    columns = d_feats_v.shape[2]
+    out_of = []
+    into = []
+    for i in range(parts):
+        span, lanes = pl.ds(i * rows, rows), pl.ds(i * columns, columns)
+        steps = (
+            (
+                d_weight.at[i // per_core, pl.ds((i % per_core) * pairs, pairs)],
+                narrow.at[i],
+                wide.at[i],
+                d_weight_out.at[span],
+            ),
+            (hid.at[span], hid_v.at[i], hid_v.at[i], hid_out.at[span]),
+            (d_feats.at[:, lanes], d_feats_v.at[i], d_feats_v.at[i], d_feats_out.at[:, lanes]),
+        )
+        for j, (here, arrive, leave, there) in enumerate(steps):
+            into.append(pltpu.make_async_copy(here, arrive, sem.at[0, 3 * i + j]))
+            out_of.append(pltpu.make_async_copy(leave, there, sem.at[1, 3 * i + j]))
+    for copy in into:
         copy.start()
     for i in range(parts):
-        into[i].wait()
-        wide[i] = narrow[i].astype(F32)
-        out_of[i].start()
-    for copy in out_of + whole:
+        for j in range(3):
+            into[3 * i + j].wait()
+            if j == 0:
+                wide[i] = narrow[i].astype(F32).reshape(rows, features)
+            out_of[3 * i + j].start()
+    for copy in out_of:
         copy.wait()
 
 
@@ -524,8 +599,9 @@
     subs = cols_x * CORES
     labels = span // subs
     half = features // CORES
-    xrows = half // cols_x
     deep = lax.axis_size("dom") // ROWS_Y
+    lanes = features // (deep // 2)
+    gather_shape = (CORES, ROWS_Y + SECOND_PAIRS, 2, TALL, features)
     vmem, smem, hbm, anywhere = (
         pl.BlockSpec(memory_space=space) for space in (pltpu.VMEM, pltpu.SMEM, pltpu.HBM, pl.ANY)
     )
@@ -542,7 +618,7 @@
         out_shape=(
             jax.ShapeDtypeStruct((features, labels), BF16),
             jax.ShapeDtypeStruct((width, span), BF16),
-            jax.ShapeDtypeStruct((features, features), BF16),
+            jax.ShapeDtypeStruct(gather_shape, BF16),
         ),
         in_specs=[smem] + [hbm] * 4,
         out_specs=(anywhere,) * 3,
@@ -566,11 +642,19 @@
             pltpu.VMEM((half, features), F32),
             pltpu.VMEM((half, features), BF16),
             pltpu.VMEM((half, features), BF16),
-            pltpu.VMEM((cols_x - 1, xrows, features), BF16),
-            pltpu.VMEM((xrows, features), BF16),
-            pltpu.VMEM((deep - 1, 16, features // 2), BF16),
-            pltpu.VMEM((ROWS_Y, 16, features // 2), BF16),
-            pltpu.VMEM((16, features // 2), BF16),
+            pltpu.VMEM((ROWS_Y - 1, 2 * TALL, features), BF16),
+            pltpu.VMEM((deep - 1, 2 * TALL, 2 * lanes), BF16),
+            pltpu.VMEM((2 * TALL, features), F32),
+            pltpu.VMEM((2 * TALL, 2 * lanes), F32),
+            pltpu.VMEM((2, TALL, features), BF16),
+            pltpu.VMEM((deep - 1, TALL, lanes), BF16),
+            pltpu.VMEM((2, TALL, 2 * lanes), BF16),
+            pltpu.VMEM((cols_x - 1, TALL, lanes), BF16),
+            pltpu.VMEM((cols_x, TALL, lanes), BF16),
+            pltpu.VMEM((ROWS_Y, TALL, lanes), BF16),
+            pltpu.VMEM((2, TALL, features), BF16),
+            pltpu.VMEM((2, TALL, 2 * lanes), BF16),
+            pltpu.VMEM(gather_shape, BF16),
             pltpu.VMEM((blocks, width, block), BF16),
             pltpu.VMEM((blocks, width, block), BF16),
             pltpu.VMEM((slots, width, block), BF16),
@@ -584,12 +668,18 @@
             dma((2, subs)),
             dma((2, subs)),
             dma((2, 1)),
+            dma((2, ROWS_Y)),
+            dma((2, deep)),
+            dma((2, cols_x)),
+            dma((2, deep)),
+            dma((2, cols_x)),
+            dma((2, ROWS_Y)),
             dma((2, cols_x)),
             dma((2, deep)),
             dma((2, ROWS_Y)),
             dma((2, deep)),
             dma((2, cols_x)),
-            dma((2, cols_x)),
+            dma((2, cols_x + 1)),
         ],
         compiler_params=pltpu.CompilerParams(
             collective_id=0, has_side_effects=True, vmem_limit_bytes=VMEM_BYTES
@@ -605,10 +695,11 @@
         in_specs=[anywhere] * 3,
         out_specs=(hbm,) * 3,
         scratch_shapes=[
-            pltpu.VMEM((4, features // 4, features), BF16),
+            pltpu.VMEM((4, features // 4, labels), BF16),
+            pltpu.VMEM((4, width, span // 4), BF16),
+            pltpu.VMEM((4, (ROWS_Y + SECOND_PAIRS) // 2, 2, TALL, features), BF16),
             pltpu.VMEM((4, features // 4, features), F32),
-            dma((2,)),
-            dma((2, 4)),
+            dma((2, 12)),
         ],
         compiler_params=pltpu.CompilerParams(vmem_limit_bytes=VMEM_BYTES),
     )(hidden, d_feats, d_weight)

time: 137 us -> 94.9 us (0.69)
  Pallas kernels: 137 us -> 94 us
    pallas_call x1, Pallas kernels: 48.8 us -> 3.12 us  [shards(): pl.pallas_call(write_kernel, out_shape=(jax.ShapeDtypeStruct((features, l...]
    pallas_call x1, Pallas kernels: 86.2 us -> 89.4 us  [shards(): pl.pallas_call(functools.partial(kernel, cols_x), out_shape=(jax.ShapeDty...]
where the time goes in v3:
time: 94.9 us; the launch traced here: 94.6 us
  Pallas kernels  94 us (99%)
    pallas_call x1, Pallas kernels, shards(): pl.pallas_call(functools.partial(kernel, cols_x), out_shape=(jax.ShapeDty...  89.4 us
    pallas_call x1, Pallas kernels, shards(): pl.pallas_call(write_kernel, out_shape=(jax.ShapeDtypeStruct((features, l...  3.12 us

profile of v3, /device:TPU:1, one launch (start us, length us, event | category | flops | bytes accessed | tf_op | source)
XLA Modules:
  0.0 94.6 jit_solution(4002753225855002450)
XLA Ops:
  0.6 1.5 %shard_map.103.plan = s32[16,128]{1,0:T(8,128)} custom-call(s32[1,4,4]{2,1,0:T(4,128)} %list_ref.1, s32[1,4]{1,0:T(1,128)} %count_ref.1, s32[1,64]{1,0:T(1,128)} %dst_ref.1, s32[1,64]{1,0:T(1,128)} %src_ref.1), custom_call_target="tpu_custom_call" | custom-call | tf_op jit(solution)/shard_map/pallas_call | solution.py:608
  2.2 89.4 %shard_map.104 = (bf16[768,512]{1,0:T(8,128)(2,1)}, bf16[96,4096]{1,0:T(8,128)(2,1)}, bf16[2,12,2,16,768]{4,3,2,1,0:T(8,128)(2,1)}) custom-call(s32[16,128]{1,0:T(8,128)} %shard_map.103.plan, bf16[96,4096]{1,0:T(8,128)(2,1)} %feats.1, bf16[768,768]{1,0:T(8,128)(2,1)} %weight.1, s32[64,128,128]{2,1,0:T(8,128)} %bitcast.1, bf16[768,512]{1,0:T(8,128)(2,1)} %cot.1), custom_call_target="tpu_custom_call" | custom-call | tf_op jit(solution)/shard_map/pallas_call | solution.py:616
  91.5 3.1 %shard_map.105 = (bf16[768,512]{1,0:T(8,128)(2,1)}, bf16[96,4096]{1,0:T(8,128)(2,1)}, f32[768,768]{1,0:T(8,128)}) custom-call(bf16[768,512]{1,0:T(8,128)(2,1)} %get-tuple-element.6.hid, bf16[96,4096]{1,0:T(8,128)(2,1)} %get-tuple-element.7.d_feats, bf16[2,12,2,16,768]{4,3,2,1,0:T(8,128)(2,1)} %get-tuple-element.8.d_weight), custom_call_target="tpu_custom_call" | custom-call | tf_op jit(solution)/shard_map/pallas_call | solution.py:688

commit v4 on v3

--- a/solution.py
+++ b/solution.py
@@ -262,10 +262,6 @@
             return carry
 
         lax.fori_loop(i * quarter, (i + 1) * quarter, halve, 0, unroll=2)
-    w_in.wait()
-    strip = features // 4
-    for i in range(4):
-        wt[:, i * strip : (i + 1) * strip] = w[i * strip : (i + 1) * strip, :].T
     for copy in sent:
         copy.wait_recv()
     table[blocks:, :width, :] = incoming[...]
@@ -302,6 +298,10 @@
         across.append(push(agg.at[s], full.at[own_rows], a2a_sem, index, dom, s))
     aggregate(sub)
     full[own_rows, :] = agg[sub]
+    w_in.wait()
+    strip = features // 4
+    for i in range(4):
+        wt[:, i * strip : (i + 1) * strip] = w[i * strip : (i + 1) * strip, :].T
     cot_in.wait()
     for copy in across:
         copy.wait_recv()
@@ -439,9 +439,12 @@
         sums[q, :width, :] = running
         return running
 
-    running = lax.fori_loop(
-        0, edges // 2, backward_edge, jnp.zeros((width, block), F32), unroll=4
-    )
+    def some_edges(i, running):
+        return lax.fori_loop(
+            i * edges // 4, (i + 1) * edges // 4, backward_edge, running, unroll=4
+        )
+
+    running = some_edges(0, jnp.zeros((width, block), F32))
     arrive(x2)
     total = second[tall_tile(x, 2)]
     for o in range(cols_x - 1):
@@ -454,7 +457,23 @@
         total = total + z2_in[o].astype(F32)
     x3_all[x] = total.astype(BF16)
     x3 = over_x(lambda i: x3_all.at[x], lambda o: x3_all.at[x], x3_sem)
-    lax.fori_loop(edges // 2, edges, backward_edge, running, unroll=4)
+    running = some_edges(1, running)
+    running = some_edges(2, running)
+    arrive(x3)
+    total = x3_all[0].astype(F32)
+    for other in range(1, cols_x):
+        total = total + x3_all[other].astype(F32)
+    mine = one_tile(z, row_z)
+    line[mine] = total.astype(BF16)
+    z4 = over_z(lambda i: line.at[mine], lambda o: line.at[mine], z4_sem)
+    arrive(y3)
+    total = y3_all[0].astype(F32)
+    for other in range(1, ROWS_Y):
+        total = total + y3_all[other].astype(F32)
+    own_tile_x = one_tile(x, 2)
+    square[own_tile_x] = total.astype(BF16)
+    x4 = over_x(lambda i: square.at[own_tile_x], lambda o: square.at[own_tile_x], x4_sem)
+    some_edges(3, running)
     home = []
     for j in range(offsets):
         for k in range(capacity):
@@ -472,27 +491,12 @@
                 sub,
             )
         )
-    arrive(x3)
-    total = x3_all[0].astype(F32)
-    for other in range(1, cols_x):
-        total = total + x3_all[other].astype(F32)
-    mine = one_tile(z, row_z)
-    line[mine] = total.astype(BF16)
-    z4 = over_z(lambda i: line.at[mine], lambda o: line.at[mine], z4_sem)
-    arrive(y3)
-    total = y3_all[0].astype(F32)
-    for other in range(1, ROWS_Y):
-        total = total + y3_all[other].astype(F32)
-    own_tile_x = one_tile(x, 2)
-    square[own_tile_x] = total.astype(BF16)
-    x4 = over_x(lambda i: square.at[own_tile_x], lambda o: square.at[own_tile_x], x4_sem)
     quarter_of = [
         (i // 2, slice(None), pl.ds(pl.multiple_of((i % 2) * wide, wide), wide))
         for i in (x, *(lax.rem(x - o + cols_x, cols_x) for o, _ in in_x))
     ]
     arrive(x4)
     square_at = (
-        core,
         ROWS_Y + z // across_z,
         slice(None),
         slice(None),
@@ -502,19 +506,26 @@
     z5 = over_z(lambda i: square, lambda o: gathered.at[square_at], z5_sem)
     arrive(z4)
     own_quarter = quarter_of[0]
-    gathered[(core, y) + own_quarter] = line[own_quarter]
+    gathered[(y,) + own_quarter] = line[own_quarter]
     y5 = over_y(
         lambda i: line.at[own_quarter],
-        lambda o: gathered.at[(core, y) + own_quarter],
+        lambda o: gathered.at[(y,) + own_quarter],
         y5_sem,
     )
 
     def all_y(quarter):
-        return gathered.at[(core, pl.ds(0, ROWS_Y)) + quarter]
+        return gathered.at[(pl.ds(0, ROWS_Y),) + quarter]
+
+    def to_results(src, at, index):
+        own_parts.append(fetch(src, d_weight.at[(core,) + at], index))
+        to_sibling.append(push(src, d_weight.at[(core,) + at], gc_sem, index, dom, sibling))
+
+    own_parts = []
+    to_sibling = []
 
     arrive(y5)
     x6 = over_x(lambda i: all_y(own_quarter), lambda o: all_y(own_quarter), x6_sem)
-    to_sibling = [push(all_y(own_quarter), all_y(own_quarter), gc_sem, 0, dom, sibling)]
+    to_results(all_y(own_quarter), (pl.ds(0, ROWS_Y),) + own_quarter, 0)
     arrive(home)
 
     def add_slot(i, running):
@@ -535,13 +546,12 @@
     lax.fori_loop(0, blocks, finish, 0, unroll=2)
     d_feats_out = fetch(result, d_feats, 8)
     arrive(z5)
-    last_rows = gathered.at[core, pl.ds(ROWS_Y, SECOND_PAIRS)]
-    to_sibling.append(push(last_rows, last_rows, gc_sem, cols_x, dom, sibling))
+    last_rows = (pl.ds(ROWS_Y, SECOND_PAIRS),)
+    to_results(gathered.at[last_rows], last_rows, cols_x)
     for (o, _), copy, quarter in zip(in_x, x6, quarter_of[1:]):
         copy.wait_recv()
-        to_sibling.append(push(all_y(quarter), all_y(quarter), gc_sem, o, dom, sibling))
+        to_results(all_y(quarter), (pl.ds(0, ROWS_Y),) + quarter, o)
     arrive(to_sibling)
-    d_weight_out = fetch(gathered, d_weight, 9)
     for copies in (
         sent, across, [to_core], backward, y1, z1, x2, z2, x3, y3, home, x4, z4, y5, z5, x6, to_sibling
     ):
@@ -549,7 +559,8 @@
             copy.wait_send()
     hid_out.wait()
     d_feats_out.wait()
-    d_weight_out.wait()
+    for copy in own_parts:
+        copy.wait()
 
 
 def write_kernel(
@@ -654,7 +665,7 @@
             pltpu.VMEM((ROWS_Y, TALL, lanes), BF16),
             pltpu.VMEM((2, TALL, features), BF16),
             pltpu.VMEM((2, TALL, 2 * lanes), BF16),
-            pltpu.VMEM(gather_shape, BF16),
+            pltpu.VMEM(gather_shape[1:], BF16),
             pltpu.VMEM((blocks, width, block), BF16),
             pltpu.VMEM((blocks, width, block), BF16),
             pltpu.VMEM((slots, width, block), BF16),

time: 94.9 us -> 94.9 us (level)
  no operation moved by 1% of the time
where the time goes in v4:
time: 94.9 us; the launch traced here: 94.6 us
  Pallas kernels  93.9 us (99%)
    pallas_call x1, Pallas kernels, shards(): pl.pallas_call(functools.partial(kernel, cols_x), out_shape=(jax.ShapeDty...  89.3 us
    pallas_call x1, Pallas kernels, shards(): pl.pallas_call(write_kernel, out_shape=(jax.ShapeDtypeStruct((features, l...  3.12 us

profile of v4, /device:TPU:1, one launch (start us, length us, event | category | flops | bytes accessed | tf_op | source)
XLA Modules:
  0.0 94.6 jit_solution(6441640618464331103)
XLA Ops:
  0.6 1.5 %shard_map.103.plan = s32[16,128]{1,0:T(8,128)} custom-call(s32[1,4,4]{2,1,0:T(4,128)} %list_ref.1, s32[1,4]{1,0:T(1,128)} %count_ref.1, s32[1,64]{1,0:T(1,128)} %dst_ref.1, s32[1,64]{1,0:T(1,128)} %src_ref.1), custom_call_target="tpu_custom_call" | custom-call | tf_op jit(solution)/shard_map/pallas_call | solution.py:619
  2.2 89.3 %shard_map.104 = (bf16[768,512]{1,0:T(8,128)(2,1)}, bf16[96,4096]{1,0:T(8,128)(2,1)}, bf16[2,12,2,16,768]{4,3,2,1,0:T(8,128)(2,1)}) custom-call(s32[16,128]{1,0:T(8,128)} %shard_map.103.plan, bf16[96,4096]{1,0:T(8,128)(2,1)} %feats.1, bf16[768,768]{1,0:T(8,128)(2,1)} %weight.1, s32[64,128,128]{2,1,0:T(8,128)} %bitcast.1, bf16[768,512]{1,0:T(8,128)(2,1)} %cot.1), custom_call_target="tpu_custom_call" | custom-call | tf_op jit(solution)/shard_map/pallas_call | solution.py:627
  91.5 3.1 %shard_map.105 = (bf16[768,512]{1,0:T(8,128)(2,1)}, bf16[96,4096]{1,0:T(8,128)(2,1)}, f32[768,768]{1,0:T(8,128)}) custom-call(bf16[768,512]{1,0:T(8,128)(2,1)} %get-tuple-element.6.hid, bf16[96,4096]{1,0:T(8,128)(2,1)} %get-tuple-element.7.d_feats, bf16[2,12,2,16,768]{4,3,2,1,0:T(8,128)(2,1)} %get-tuple-element.8.d_weight), custom_call_target="tpu_custom_call" | custom-call | tf_op jit(solution)/shard_map/pallas_call | solution.py:699

commit v5 on v2

--- a/solution.py
+++ b/solution.py
@@ -110,6 +110,7 @@
     z_in,
     y_all,
     summed,
+    gathered,
     back,
     scaled,
     returning,
@@ -245,10 +246,6 @@
             return carry
 
         lax.fori_loop(i * quarter, (i + 1) * quarter, halve, 0, unroll=2)
-    w_in.wait()
-    strip = features // 4
-    for i in range(4):
-        wt[:, i * strip : (i + 1) * strip] = w[i * strip : (i + 1) * strip, :].T
     for copy in sent:
         copy.wait_recv()
     table[blocks:, :width, :] = incoming[...]
@@ -285,6 +282,10 @@
         across.append(push(agg.at[s], full.at[own_rows], a2a_sem, index, dom, s))
     aggregate(sub)
     full[own_rows, :] = agg[sub]
+    w_in.wait()
+    strip = features // 4
+    for i in range(4):
+        wt[:, i * strip : (i + 1) * strip] = w[i * strip : (i + 1) * strip, :].T
     cot_in.wait()
     for copy in across:
         copy.wait_recv()
@@ -397,9 +398,9 @@
         pl.ds(pl.multiple_of((z % 2) * wide, wide), wide),
     )
     over_z = [
-        push(summed, d_weight.at[mine], gz_sem, o, other * ROWS_Y + y, sub) for o, other in in_z
-    ]
-    own_piece = fetch(summed, d_weight.at[mine], 0)
+        push(summed, gathered.at[mine], gz_sem, o, other * ROWS_Y + y, sub) for o, other in in_z
+    ]
+    gathered[mine] = summed[...]
     for copy in backward:
         copy.wait_recv()
 
@@ -436,12 +437,20 @@
         )
     for copy in over_z:
         copy.wait_recv()
-    own_piece.wait()
-    strip_x = d_weight.at[x_strip(core, x)]
+    def to_results(of_x, index):
+        rows = x_strip(core, of_x)
+        own_parts.append(fetch(gathered.at[rows], d_weight.at[rows], index))
+        over_core.append(
+            push(gathered.at[rows], d_weight.at[rows], gc_sem, index, dom, sibling)
+        )
+
+    own_parts = []
+    over_core = []
+    strip_x = gathered.at[x_strip(core, x)]
     over_x = [
         push(strip_x, strip_x, gx_sem, o, dom, other * CORES + core) for o, other in in_x
     ]
-    over_core = [push(strip_x, strip_x, gc_sem, 0, dom, sibling)]
+    to_results(x, 0)
     for copy in home:
         copy.wait_recv()
 
@@ -464,8 +473,7 @@
     d_feats_out = fetch(result, d_feats, 8)
     for (o, _), copy in zip(in_x, over_x):
         copy.wait_recv()
-        arrived = d_weight.at[x_strip(core, lax.rem(x - o + cols_x, cols_x))]
-        over_core.append(push(arrived, arrived, gc_sem, o, dom, sibling))
+        to_results(lax.rem(x - o + cols_x, cols_x), o)
     for copy in over_core:
         copy.wait_recv()
     for copy in (
@@ -484,32 +492,36 @@
         copy.wait_send()
     hid_out.wait()
     d_feats_out.wait()
+    for copy in own_parts:
+        copy.wait()
 
 
 def write_kernel(
-    hid, d_feats, d_weight, hid_out, d_feats_out, d_weight_out, narrow, wide, sem, part_sem
+    hid, d_feats, d_weight, hid_out, d_feats_out, d_weight_out, hid_v, d_feats_v, narrow, wide, sem
 ):
     parts, rows, _ = narrow.shape
-    whole = [
-        pltpu.make_async_copy(hid, hid_out, sem.at[0]),
-        pltpu.make_async_copy(d_feats, d_feats_out, sem.at[1]),
-    ]
-    spans = [pl.ds(i * rows, rows) for i in range(parts)]
-    into = [
-        pltpu.make_async_copy(d_weight.at[spans[i]], narrow.at[i], part_sem.at[0, i])
-        for i in range(parts)
-    ]
-    out_of = [
-        pltpu.make_async_copy(wide.at[i], d_weight_out.at[spans[i]], part_sem.at[1, i])
-        for i in range(parts)
-    ]
-    for copy in into + whole:
+    columns = d_feats_v.shape[2]
+    out_of = []
+    into = []
+    for i in range(parts):
+        span, lanes = pl.ds(i * rows, rows), pl.ds(i * columns, columns)
+        steps = (
+            (d_weight.at[span], narrow.at[i], wide.at[i], d_weight_out.at[span]),
+            (hid.at[span], hid_v.at[i], hid_v.at[i], hid_out.at[span]),
+            (d_feats.at[:, lanes], d_feats_v.at[i], d_feats_v.at[i], d_feats_out.at[:, lanes]),
+        )
+        for j, (here, arrive, leave, there) in enumerate(steps):
+            into.append(pltpu.make_async_copy(here, arrive, sem.at[0, 3 * i + j]))
+            out_of.append(pltpu.make_async_copy(leave, there, sem.at[1, 3 * i + j]))
+    for copy in into:
         copy.start()
     for i in range(parts):
-        into[i].wait()
-        wide[i] = narrow[i].astype(F32)
-        out_of[i].start()
-    for copy in out_of + whole:
+        for j in range(3):
+            into[3 * i + j].wait()
+            if j == 0:
+                wide[i] = narrow[i].astype(F32)
+            out_of[3 * i + j].start()
+    for copy in out_of:
         copy.wait()
 
 
@@ -571,6 +583,7 @@
             pltpu.VMEM((deep - 1, 16, features // 2), BF16),
             pltpu.VMEM((ROWS_Y, 16, features // 2), BF16),
             pltpu.VMEM((16, features // 2), BF16),
+            pltpu.VMEM((features, features), BF16),
             pltpu.VMEM((blocks, width, block), BF16),
             pltpu.VMEM((blocks, width, block), BF16),
             pltpu.VMEM((slots, width, block), BF16),
@@ -605,10 +618,11 @@
         in_specs=[anywhere] * 3,
         out_specs=(hbm,) * 3,
         scratch_shapes=[
+            pltpu.VMEM((4, features // 4, labels), BF16),
+            pltpu.VMEM((4, width, span // 4), BF16),
             pltpu.VMEM((4, features // 4, features), BF16),
             pltpu.VMEM((4, features // 4, features), F32),
-            dma((2,)),
-            dma((2, 4)),
+            dma((2, 12)),
         ],
         compiler_params=pltpu.CompilerParams(vmem_limit_bytes=VMEM_BYTES),
     )(hidden, d_feats, d_weight)

time: 137 us -> 91.1 us (0.66)
  Pallas kernels: 137 us -> 90.2 us
    pallas_call x1, Pallas kernels: 48.8 us -> 3.12 us  [shards(): pl.pallas_call(write_kernel, out_shape=(jax.ShapeDtypeStruct((features, l...]
where the time goes in v5:
time: 91.1 us; the launch traced here: 90.8 us
  Pallas kernels  90.2 us (99%)
    pallas_call x1, Pallas kernels, shards(): pl.pallas_call(functools.partial(kernel, cols_x), out_shape=(jax.ShapeDty...  85.6 us
    pallas_call x1, Pallas kernels, shards(): pl.pallas_call(write_kernel, out_shape=(jax.ShapeDtypeStruct((features, l...  3.12 us

profile of v5, /device:TPU:1, one launch (start us, length us, event | category | flops | bytes accessed | tf_op | source)
XLA Modules:
  0.0 90.8 jit_solution(2723572074705080930)
XLA Ops:
  0.6 1.5 %shard_map.103.plan = s32[16,128]{1,0:T(8,128)} custom-call(s32[1,4,4]{2,1,0:T(4,128)} %list_ref.1, s32[1,4]{1,0:T(1,128)} %count_ref.1, s32[1,64]{1,0:T(1,128)} %dst_ref.1, s32[1,64]{1,0:T(1,128)} %src_ref.1), custom_call_target="tpu_custom_call" | custom-call | tf_op jit(solution)/shard_map/pallas_call | solution.py:544
  2.2 85.6 %shard_map.104 = (bf16[768,512]{1,0:T(8,128)(2,1)}, bf16[96,4096]{1,0:T(8,128)(2,1)}, bf16[768,768]{1,0:T(8,128)(2,1)}) custom-call(s32[16,128]{1,0:T(8,128)} %shard_map.103.plan, bf16[96,4096]{1,0:T(8,128)(2,1)} %feats.1, bf16[768,768]{1,0:T(8,128)(2,1)} %weight.1, s32[64,128,128]{2,1,0:T(8,128)} %bitcast.1, bf16[768,512]{1,0:T(8,128)(2,1)} %cot.1), custom_call_target="tpu_custom_call" | custom-call | tf_op jit(solution)/shard_map/pallas_call | solution.py:552
  87.7 3.1 %shard_map.105 = (bf16[768,512]{1,0:T(8,128)(2,1)}, bf16[96,4096]{1,0:T(8,128)(2,1)}, f32[768,768]{1,0:T(8,128)}) custom-call(bf16[768,512]{1,0:T(8,128)(2,1)} %get-tuple-element.6.hid, bf16[96,4096]{1,0:T(8,128)(2,1)} %get-tuple-element.7.d_feats, bf16[768,768]{1,0:T(8,128)(2,1)} %get-tuple-element.8.d_weight), custom_call_target="tpu_custom_call" | custom-call | tf_op jit(solution)/shard_map/pallas_call | solution.py:611

commit v6 on v5

--- a/solution.py
+++ b/solution.py
@@ -116,6 +116,7 @@
     returning,
     returned,
     slot_sums,
+    base,
     result,
     local_sem,
     tile_sem,
@@ -204,13 +205,6 @@
             barrier, inc=1, device_id=partner, device_id_type=pl.DeviceIdType.MESH
         )
 
-    quarter = edges // 4
-    mask_in = [
-        fetch(mask.at[pl.ds(i * quarter, quarter)], mask_int.at[pl.ds(i * quarter, quarter)], 1 + i)
-        for i in range(4)
-    ]
-    w_in = fetch(weight, w, 5)
-    cot_in = fetch(cot, cot_v, 6)
 
     def ones_below(t, carry):
         table[t, width:, :] = jnp.ones((ONES, block), BF16)
@@ -236,8 +230,15 @@
             in_dom[j],
             sub,
         )
-        for j in range(offsets)
-    ]
+        for j in reversed(range(offsets))
+    ]
+    quarter = edges // 4
+    mask_in = [
+        fetch(mask.at[pl.ds(i * quarter, quarter)], mask_int.at[pl.ds(i * quarter, quarter)], 1 + i)
+        for i in range(4)
+    ]
+    w_in = fetch(weight, w, 5)
+    cot_in = fetch(cot, cot_v, 6)
     for i in range(4):
         mask_in[i].wait()
 
@@ -261,7 +262,7 @@
         sums[q] = running
         return running
 
-    lax.fori_loop(0, edges, forward, jnp.zeros((width + ONES, block), F32), unroll=4)
+    lax.fori_loop(0, edges, forward, jnp.zeros((width + ONES, block), F32), unroll=16)
 
     def aggregate(s):
         def one(i, carry):
@@ -320,20 +321,6 @@
     def x_rows(i):
         return pl.ds(pl.multiple_of(i * xrows, xrows), xrows)
 
-    to_core.wait_recv()
-
-    def add_core(i, carry):
-        total = dw_own[x_rows(i), :] + core_in[x_rows(i), :].astype(F32)
-        dw_own[x_rows(i), :] = total
-        x_out[x_rows(i), :] = total.astype(BF16)
-        return carry
-
-    lax.fori_loop(0, cols_x, add_core, 0)
-    to_x = [
-        push(x_out.at[x_rows(other)], x_in.at[o - 1], x_sem, o, dom, other * CORES + core)
-        for o, other in in_x
-    ]
-
     def gradient(i, carry):
         rows = half_rows(i)
         product = jnp.dot(wt[rows, :], d_pre[...], preferred_element_type=F32).astype(BF16)
@@ -343,23 +330,22 @@
 
     lax.fori_loop(0, CORES, gradient, 0)
 
-    def z_part(i):
-        return (
-            pl.ds(pl.multiple_of((i // 2) * 16, 16), 16),
-            pl.ds(pl.multiple_of((i % 2) * wide, wide), wide),
-        )
-
-    for copy in to_x:
-        copy.wait_recv()
-    total = dw_own[x_rows(x), :]
-    for o in range(cols_x - 1):
-        total = total + x_in[o].astype(F32)
-    dw_own[:xrows, :] = total
-    z_out[...] = total.astype(BF16)
-    to_z = [
-        push(z_out.at[z_part(other)], z_in.at[o - 1], z_sem, o, other * ROWS_Y + y, sub)
-        for o, other in in_z
-    ]
+    to_core.wait_recv()
+
+    def add_core(i):
+        total = dw_own[x_rows(i), :] + core_in[x_rows(i), :].astype(F32)
+        dw_own[x_rows(i), :] = total
+        x_out[x_rows(i), :] = total.astype(BF16)
+
+    to_x = []
+    for o, other in in_x:
+        add_core(other)
+        to_x.append(
+            push(x_out.at[x_rows(other)], x_in.at[o - 1], x_sem, o, dom, other * CORES + core)
+        )
+    add_core(x)
+
+
     own_blocks = pl.ds(sub * per_sub, per_sub)
     backward = [
         push(
@@ -373,6 +359,24 @@
         for index, s in in_sub
     ]
     back[own_blocks] = d_agg[:, own_rows, :]
+
+    def z_part(i):
+        return (
+            pl.ds(pl.multiple_of((i // 2) * 16, 16), 16),
+            pl.ds(pl.multiple_of((i % 2) * wide, wide), wide),
+        )
+
+    for copy in to_x:
+        copy.wait_recv()
+    total = dw_own[x_rows(x), :]
+    for o in range(cols_x - 1):
+        total = total + x_in[o].astype(F32)
+    dw_own[:xrows, :] = total
+    z_out[...] = total.astype(BF16)
+    to_z = [
+        push(z_out.at[z_part(other)], z_in.at[o - 1], z_sem, o, other * ROWS_Y + y, sub)
+        for o, other in in_z
+    ]
     for copy in to_z:
         copy.wait_recv()
     rows, columns = z_part(z)
@@ -383,6 +387,29 @@
     to_y = [
         push(y_all.at[y], y_all.at[y], y_sem, o, z * ROWS_Y + other, sub) for o, other in in_y
     ]
+    for copy in backward:
+        copy.wait_recv()
+
+    def rescale(b, carry):
+        scaled[b] = (back[b].astype(F32) * scales[b][:1]).astype(BF16)
+        return carry
+
+    lax.fori_loop(0, blocks, rescale, 0, unroll=2)
+
+    def backward_edge(q, running):
+        product = jnp.dot(scaled[plan[6, q]], mask_half[plan[5, q]], preferred_element_type=F32)
+        running = running * plan[7, q].astype(F32) + product
+        sums[q, :width, :] = running
+        return running
+
+    def some_edges(i, running):
+        return lax.fori_loop(
+            i * edges // 4, (i + 1) * edges // 4, backward_edge, running, unroll=16
+        )
+
+    running = jnp.zeros((width, block), F32)
+    for part in range(1):
+        running = some_edges(part, running)
     for copy in to_y:
         copy.wait_recv()
     total = y_all[0].astype(F32)
@@ -401,25 +428,10 @@
         push(summed, gathered.at[mine], gz_sem, o, other * ROWS_Y + y, sub) for o, other in in_z
     ]
     gathered[mine] = summed[...]
-    for copy in backward:
-        copy.wait_recv()
-
-    def rescale(b, carry):
-        scaled[b] = (back[b].astype(F32) * scales[b][:1]).astype(BF16)
-        return carry
-
-    lax.fori_loop(0, blocks, rescale, 0, unroll=2)
-    def backward_edge(q, running):
-        product = jnp.dot(
-            scaled[plan[6, q]], mask_half[plan[5, q]], preferred_element_type=F32
-        )
-        running = running * plan[7, q].astype(F32) + product
-        sums[q, :width, :] = running
-        return running
-
-    lax.fori_loop(0, edges, backward_edge, jnp.zeros((width, block), F32), unroll=4)
+    for part in range(1, 4):
+        running = some_edges(part, running)
     home = []
-    for j in range(offsets):
+    for j in reversed(range(offsets)):
         for k in range(capacity):
             t = blocks + j * capacity + k
             returning[j * capacity + k] = (
@@ -451,6 +463,11 @@
         push(strip_x, strip_x, gx_sem, o, dom, other * CORES + core) for o, other in in_x
     ]
     to_results(x, 0)
+    def own_total(b, carry):
+        base[b] = scaled[b].astype(F32) + sums[plan[8, b]][:width] * plan[9, b].astype(F32)
+        return carry
+
+    lax.fori_loop(0, blocks, own_total, 0, unroll=2)
     for copy in home:
         copy.wait_recv()
 
@@ -463,8 +480,7 @@
 
     def finish(b, carry):
         result[:, tile(b)] = (
-            scaled[b].astype(F32)
-            + sums[plan[8, b]][:width] * plan[9, b].astype(F32)
+            base[b]
             + slot_sums[plan[13, b]] * plan[14, b].astype(F32)
         ).astype(BF16)
         return carry
@@ -589,6 +605,7 @@
             pltpu.VMEM((slots, width, block), BF16),
             pltpu.VMEM((slots, width, block), BF16),
             pltpu.VMEM((slots, width, block), F32),
+            pltpu.VMEM((blocks, width, block), F32),
             pltpu.VMEM((width, span), BF16),
             dma((10,)),
             dma((blocks,)),

time: 91.1 us -> 90.7 us (level)
  no operation moved by 1% of the time
where the time goes in v6:
time: 90.7 us; the launch traced here: 90.5 us
  Pallas kernels  89.9 us (99%)
    pallas_call x1, Pallas kernels, shards(): pl.pallas_call(functools.partial(kernel, cols_x), out_shape=(jax.ShapeDty...  85.2 us
    pallas_call x1, Pallas kernels, shards(): pl.pallas_call(write_kernel, out_shape=(jax.ShapeDtypeStruct((features, l...  3.12 us

profile of v6, /device:TPU:1, one launch (start us, length us, event | category | flops | bytes accessed | tf_op | source)
XLA Modules:
  0.0 90.5 jit_solution(2582447299369217396)
XLA Ops:
  0.6 1.5 %shard_map.103.plan = s32[16,128]{1,0:T(8,128)} custom-call(s32[1,4,4]{2,1,0:T(4,128)} %list_ref.1, s32[1,4]{1,0:T(1,128)} %count_ref.1, s32[1,64]{1,0:T(1,128)} %dst_ref.1, s32[1,64]{1,0:T(1,128)} %src_ref.1), custom_call_target="tpu_custom_call" | custom-call | tf_op jit(solution)/shard_map/pallas_call | solution.py:560
  2.2 85.2 %shard_map.104 = (bf16[768,512]{1,0:T(8,128)(2,1)}, bf16[96,4096]{1,0:T(8,128)(2,1)}, bf16[768,768]{1,0:T(8,128)(2,1)}) custom-call(s32[16,128]{1,0:T(8,128)} %shard_map.103.plan, bf16[96,4096]{1,0:T(8,128)(2,1)} %feats.1, bf16[768,768]{1,0:T(8,128)(2,1)} %weight.1, s32[64,128,128]{2,1,0:T(8,128)} %bitcast.1, bf16[768,512]{1,0:T(8,128)(2,1)} %cot.1), custom_call_target="tpu_custom_call" | custom-call | tf_op jit(solution)/shard_map/pallas_call | solution.py:568
  87.4 3.1 %shard_map.105 = (bf16[768,512]{1,0:T(8,128)(2,1)}, bf16[96,4096]{1,0:T(8,128)(2,1)}, f32[768,768]{1,0:T(8,128)}) custom-call(bf16[768,512]{1,0:T(8,128)(2,1)} %get-tuple-element.6.hid, bf16[96,4096]{1,0:T(8,128)(2,1)} %get-tuple-element.7.d_feats, bf16[768,768]{1,0:T(8,128)(2,1)} %get-tuple-element.8.d_weight), custom_call_target="tpu_custom_call" | custom-call | tf_op jit(solution)/shard_map/pallas_call | solution.py:628
